TPU v7x, 32 devices: a whole 2x2x4 slice. The times are simulated.
32 devices in a mesh: parts: 2 (over y), seq: 4 (over z), head: 2 (over x), hgt: 2 (over core).
Axes of the slice: x: 2, y: 2, z: 4, core: 2. Of those that a mesh axis runs over, the one named last changes fastest.
Arguments:
- queries: bfloat16 [16, 8, 24, 2048], P(('parts', 'seq'), 'hgt', None, 'head'), parts along dimension 0
- key_rows: bfloat16 [16, 8, 24, 2048], P(('parts', 'seq'), 'hgt', None, 'head'), parts along dimension 0
- value_rows: bfloat16 [16, 8, 24, 2048], P(('parts', 'seq'), 'hgt', None, 'head'), parts along dimension 0, may hold values from -6 to 6
- out_grad: bfloat16 [16, 8, 24, 3072], P(('parts', 'seq'), 'hgt', None, 'head'), parts along dimension 0, may hold values from -6 to 6
- w_out: bfloat16 [3072, 2048], P(None, 'head'), may hold values from -0.109375 to 0.109375
- text_keys: bfloat16 [512, 2048], P('parts', 'head'), parts along dimension 0, may hold values from -6 to 6
- text_values: bfloat16 [512, 2048], P('parts', 'head'), parts along dimension 0, may hold values from -6 to 6
- text_count: int32 [2], P('parts'), parts along dimension 0, may hold values from 64 to 256
- window_start: int32 [16, 4, 3, 3], P('parts'), parts along dimension 0, may hold values from 0 to 5, as said below
Outputs:
- grad_query: bfloat16 [16, 8, 24, 2048], P(('parts', 'seq'), 'hgt', None, 'head'), parts along dimension 0
- grad_key: bfloat16 [16, 8, 24, 2048], P(('parts', 'seq'), 'hgt', None, 'head'), parts along dimension 0
- grad_value: bfloat16 [16, 8, 24, 2048], P(('parts', 'seq'), 'hgt', None, 'head'), parts along dimension 0
- grad_w_out: float32 [6144, 2048], P(('parts', 'seq', 'hgt'), 'head'), parts along dimension 0
- grad_text_key: float32 [512, 2048], P('parts', 'head'), parts along dimension 0
- grad_text_value: float32 [512, 2048], P('parts', 'head'), parts along dimension 0
There are 2 independent parts, one for each index of `parts`. A program takes and returns all parts, laid end to end along the dimension named above; an argument that names none is the same for every part. Nothing has to cross between parts.
Inputs may be any that keep to these rules, and one draw needn't show every extreme that they name: window_start[a, b, c] names the first frame, height tile and width tile of the window of the tile at frame a, height tile b, width tile c; each window lies inside the clip and contains that tile. The first text_count[0] text slots are valid.
All inputs are finite; a program needn't handle non-finite values.
Results may differ from a plain program's by a relative error of at most 0.012.
Values may be sent and summed in bfloat16 or wider, within the bound.
A program may use at most 128 MiB of HBM per device.

v0:
```python
import jax
import jax.numpy as jnp
from jax import lax
from jax.sharding import PartitionSpec as P

HDIM = 128
TH = 2
TW = 8
WIN = 3


def with_halo(block, sides, width):
    for axis, dim in sides:
        count = lax.axis_size(axis)
        forward = [(i, i + 1) for i in range(count - 1)]
        backward = [(target, source) for source, target in forward]
        low = lax.ppermute(
            lax.slice_in_dim(block, block.shape[dim] - width, None, axis=dim), axis, forward
        )
        high = lax.ppermute(lax.slice_in_dim(block, 0, width, axis=dim), axis, backward)
        block = jnp.concatenate([low, block, high], axis=dim)
    return block


def from_behind(block, axis, distance):
    devices = range(lax.axis_size(axis))
    route = [(i - distance, i) for i in devices if i - distance in devices]
    return lax.ppermute(block, axis, route)


def swapped(block, axis, stride):
    count = lax.axis_size(axis)
    route = []
    for low in range(count):
        high = low | 1 << stride
        if high != low and high < count:
            route += [(low, high), (high, low)]
    return lax.ppermute(block, axis, route)


def window_test(lower_f, lower_r, lower_c, key_frame, key_row, key_col):
    tile_row = key_row // TH
    tile_col = key_col // TW
    return (
        (key_frame >= lower_f)
        & (key_frame < lower_f + WIN)
        & (tile_row >= lower_r)
        & (tile_row < lower_r + WIN)
        & (tile_col >= lower_c)
        & (tile_col < lower_c + WIN)
    )


def query_side(
    query_h, key_h, value_h, text_key_h, text_value_h, grad_h, allowed, text_open, score_scale
):
    score_w = (
        jnp.einsum("qd,kd->qk", query_h, key_h, preferred_element_type=jnp.float32) * score_scale
    )
    score_t = (
        jnp.einsum("qd,kd->qk", query_h, text_key_h, preferred_element_type=jnp.float32)
        * score_scale
    )
    score_w = jnp.where(allowed, score_w, -jnp.inf)
    score_t = jnp.where(text_open, score_t, -jnp.inf)
    row_top = jnp.maximum(jnp.max(score_w, axis=1), jnp.max(score_t, axis=1))
    total = jnp.sum(jnp.exp(score_w - row_top[:, None]), axis=1) + jnp.sum(
        jnp.exp(score_t - row_top[:, None]), axis=1
    )
    log_total = row_top + jnp.log(total)
    prob_w = jnp.exp(score_w - log_total[:, None])
    prob_t = jnp.exp(score_t - log_total[:, None])
    pb_w = prob_w.astype(jnp.bfloat16)
    pb_t = prob_t.astype(jnp.bfloat16)
    attn_out = (
        jnp.dot(pb_w, value_h, preferred_element_type=jnp.float32)
        + jnp.dot(pb_t, text_value_h, preferred_element_type=jnp.float32)
    ).astype(jnp.bfloat16)
    row_delta = jnp.sum(grad_h.astype(jnp.float32) * attn_out.astype(jnp.float32), axis=1)
    dp_w = jnp.einsum("qd,kd->qk", grad_h, value_h, preferred_element_type=jnp.float32)
    dp_t = jnp.einsum("qd,kd->qk", grad_h, text_value_h, preferred_element_type=jnp.float32)
    ds_w = (prob_w * (dp_w - row_delta[:, None])).astype(jnp.bfloat16)
    ds_t = (prob_t * (dp_t - row_delta[:, None])).astype(jnp.bfloat16)
    grad_q = (
        (
            jnp.dot(ds_w, key_h, preferred_element_type=jnp.float32)
            + jnp.dot(ds_t, text_key_h, preferred_element_type=jnp.float32)
        )
        * score_scale
    ).astype(jnp.bfloat16)
    grad_tk = (
        jnp.einsum("qk,qd->kd", ds_t, query_h, preferred_element_type=jnp.float32) * score_scale
    )
    grad_tv = jnp.einsum("qk,qd->kd", pb_t, grad_h, preferred_element_type=jnp.float32)
    result = [grad_q, attn_out, log_total, row_delta, grad_tk, grad_tv]
    result.append(
        jnp.einsum("qk,qd->kd", ds_w, query_h, preferred_element_type=jnp.float32) * score_scale
    )
    result.append(jnp.einsum("qk,qd->kd", pb_w, grad_h, preferred_element_type=jnp.float32))
    return result


def per_device(
    queries, key_rows, value_rows, out_grad, w_out, text_keys, text_values, text_count, window_start
):
    frames, height, col_count, columns = queries.shape
    head_count = columns // HDIM
    row_count = frames * height * col_count
    score_scale = jnp.float32(HDIM ** (-0.5))
    hgt_count = lax.axis_size("hgt")
    full_h = height * hgt_count
    frame_first = lax.axis_index("seq") * frames
    row_first = lax.axis_index("hgt") * height
    grad_full = lax.all_gather(out_grad.reshape(row_count, -1), "head", axis=1, tiled=True)
    grad_o = jnp.dot(grad_full, w_out, preferred_element_type=jnp.float32).astype(jnp.bfloat16)
    key_value = jnp.concatenate([key_rows, value_rows], axis=3)
    key_value = lax.all_gather(key_value, "hgt", axis=1, tiled=True)
    extended = with_halo(key_value, (("seq", 0),), frames)
    ext_rows = extended.reshape(-1, 2 * columns)
    tiles_h = full_h // TH
    tiles_w = col_count // TW
    start_table = window_start.reshape(-1, 3)
    own_index = jnp.arange(row_count, dtype=jnp.int32)
    own_frame = frame_first + own_index // (height * col_count)
    own_row = row_first + own_index // col_count % height
    own_col = own_index % col_count
    own_tile = own_frame * (tiles_h * tiles_w) + own_row // TH * tiles_w + own_col // TW
    own_start = jnp.take(start_table, own_tile, axis=0)
    ext_count = ext_rows.shape[0]
    ext_index = jnp.arange(ext_count, dtype=jnp.int32)
    ext_frame = frame_first - frames + ext_index // (full_h * col_count)
    ext_row = ext_index // col_count % full_h
    ext_col = ext_index % col_count
    allowed = window_test(
        own_start[:, 0:1],
        own_start[:, 1:2],
        own_start[:, 2:3],
        ext_frame[None, :],
        ext_row[None, :],
        ext_col[None, :],
    )
    text_open = (jnp.arange(text_keys.shape[0], dtype=jnp.int32) < text_count[0])[None, :]
    query_flat = queries.reshape(row_count, columns)
    results = []
    for head_num in range(head_count):
        low = head_num * HDIM
        high = low + HDIM
        results.append(
            query_side(
                query_flat[:, low:high],
                ext_rows[:, low:high],
                ext_rows[:, columns + low : columns + high],
                text_keys[:, low:high],
                text_values[:, low:high],
                grad_o[:, low:high],
                allowed,
                text_open,
                score_scale,
            )
        )
    grad_query = jnp.concatenate([item[0] for item in results], axis=1).reshape(queries.shape)
    attn_all = jnp.concatenate([item[1] for item in results], axis=1)
    text_gk = jnp.concatenate([item[4] for item in results], axis=1)
    text_gv = jnp.concatenate([item[5] for item in results], axis=1)
    key_part = jnp.concatenate([item[6] for item in results], axis=1)
    value_part = jnp.concatenate([item[7] for item in results], axis=1)
    contrib = jnp.concatenate([key_part, value_part], axis=1).reshape(
        3 * frames, full_h, col_count, 2 * columns
    )
    from_upper = from_behind(contrib[:frames], "seq", -1)
    from_lower = from_behind(contrib[2 * frames :], "seq", 1)
    own_part = contrib[frames : 2 * frames] + from_upper + from_lower
    mine = lax.dynamic_slice_in_dim(own_part, row_first, height, 1)
    other = lax.dynamic_slice_in_dim(own_part, (1 - lax.axis_index("hgt")) * height, height, 1)
    mine = mine + swapped(other, "hgt", 0)
    grad_key = mine[..., :columns].astype(jnp.bfloat16)
    grad_value = mine[..., columns:].astype(jnp.bfloat16)
    grad_text_key, grad_text_value = lax.psum((text_gk, text_gv), ("seq", "hgt"))
    grad_w_out = lax.psum_scatter(
        lax.dot_general(
            grad_full, attn_all, (((0,), (0,)), ((), ())), preferred_element_type=jnp.float32
        ),
        ("seq", "hgt"),
        scatter_dimension=0,
        tiled=True,
    )
    return (grad_query, grad_key, grad_value, grad_w_out, grad_text_key, grad_text_value)


def solution(mesh):
    placed = (
        P(("parts", "seq"), "hgt", None, "head"),
        P(("parts", "seq"), "hgt", None, "head"),
        P(("parts", "seq"), "hgt", None, "head"),
        P(("parts", "seq"), "hgt", None, "head"),
        P(None, "head"),
        P("parts", "head"),
        P("parts", "head"),
        P("parts"),
        P("parts", None, None, None),
    )
    return jax.shard_map(
        per_device,
        mesh=mesh,
        in_specs=placed,
        out_specs=(
            P(("parts", "seq"), "hgt", None, "head"),
            P(("parts", "seq"), "hgt", None, "head"),
            P(("parts", "seq"), "hgt", None, "head"),
            P(("parts", "seq", "hgt"), "head"),
            P("parts", "head"),
            P("parts", "head"),
        ),
        check_vma=False,
    )
```

profile of v0, /device:TPU:0, one launch (start us, length us, event | category | flops | bytes accessed | tf_op | source)
XLA Modules:
  0.0 357.8 jit_solution(12289085791843155510)
XLA Ops:
  7.2 2.1 pad_maximum_fusion.1
  11.2 2.3 fusion.347
  13.5 2.3 fusion.349
  15.8 2.3 fusion.351
  18.1 2.3 fusion.353
  22.7 1.3 collective-permute-start.1
  24.0 6.4 %collective-permute-start = (bf16[2,8,24,2048]{3,2,1,0:T(8,128)(2,1)}, bf16[2,8,24,2048]{3,2,1,0:T(8,128)(2,1)}, u32[]{:S(2)}, u32[]{:S(2)}) collective-permute-start(bf16[2,8,24,2048]{3,2,1,0:T(8,128)(2,1)} %all-gather.3.cloned.1.call-done), channel_id=1, source_target_pairs={{0,4},{4,8},{8,12},{1,5},{5,9},{9,13},{2,6},{6,10},{10,14},{3,7},{... | collective-permute-start | bytes 4718600 | tf_op jit(solution)/shard_map/ppermute | solution.py:17
  30.9 1.5 fusion.355
  32.3 1.4 fusion.357
  33.7 1.4 fusion.359
  35.2 1.4 fusion.345
  36.6 11.6 %all-gather.5.cloned.1.call-done = bf16[192,3072]{1,0:T(8,128)(2,1)} async-done(((bf16[192,1536]{1,0:T(8,128)(2,1)}), bf16[192,3072]{1,0:T(8,128)(2,1)}) %all-gather.5.cloned.1.call-update) | async-done | bytes 1179664 | tf_op jit(solution)/shard_map/all_gather | solution.py:114
  48.2 4.5 %convolution_convert_fusion = bf16[192,1024]{1,0:T(8,128)(2,1)S(1)} fusion(bf16[192,3072]{1,0:T(8,128)(2,1)} %all-gather.5.cloned.1.call-done, bf16[3072,1024]{1,0:T(8,128)(2,1)} %param.13), kind=kOutput, calls=%fused_computation.77 | convolution fusion | flops 1208156160 | bytes 7864320 | tf_op jit(solution)/shard_map/dot_general | solution.py:115
  52.8 9.2 %collective-permute-done.1 = bf16[2,8,24,2048]{3,2,1,0:T(8,128)(2,1)} collective-permute-done((bf16[2,8,24,2048]{3,2,1,0:T(8,128)(2,1)}, bf16[2,8,24,2048]{3,2,1,0:T(8,128)(2,1)}, u32[]{:S(2)}, u32[]{:S(2)}) %collective-permute-start.1) | collective-permute-done | bytes 1572896 | tf_op jit(solution)/shard_map/ppermute | solution.py:20
  63.2 2.3 pad_maximum_fusion
  68.4 1.4 fusion.352
  69.9 1.4 fusion.350
  94.8 1.4 constant_dynamic-update-slice_fusion
  96.3 7.8 %convolution_bitcast_fusion = f32[3072,1024]{0,1:T(8,128)} fusion(bf16[192,1024]{1,0:T(8,128)(2,1)} %constant_dynamic-update-slice_fusion, bf16[192,3072]{1,0:T(8,128)(2,1)} %all-gather.5.cloned.1.call-done), kind=kOutput, calls=%fused_computation.1 | convolution fusion | flops 1207959552 | bytes 14155776 | tf_op jit(solution)/shard_map/dot_general | solution.py:180
  104.2 1.7 fusion.32
  107.0 1.6 fusion.33
  109.9 1.2 fusion.34
  111.9 1.2 fusion.35
  113.5 1.4 fusion.36
  116.0 1.3 fusion.37
  117.6 1.3 fusion.38
  119.2 1.3 fusion.39
  124.0 3.4 fusion.342
  127.4 3.6 %copy.25 = f32[384,2048]{1,0:T(8,128)} copy(f32[384,2048]{0,1:T(8,128)} %get-tuple-element.34) | data formatting | bytes 6291456 | tf_op jit(solution)/shard_map/slice | solution.py:170
  131.0 3.6 %copy.26 = f32[384,2048]{1,0:T(8,128)} copy(f32[384,2048]{0,1:T(8,128)} %get-tuple-element.35) | data formatting | bytes 6291456 | tf_op jit(solution)/shard_map/slice | solution.py:171
  134.6 6.2 %collective-permute-start.3 = (f32[2,8,24,2048]{3,2,1,0:T(8,128)}, f32[2,8,24,2048]{3,2,1,0:T(8,128)}, u32[]{:S(2)}, u32[]{:S(2)}) collective-permute-start(f32[2,8,24,2048]{3,2,1,0:T(8,128)} %bitcast.147), channel_id=1, source_target_pairs={{0,4},{4,8},{8,12},{1,5},{5,9},{9,13},{2,6},{6,10},{10,14},{3,7},{... | collective-permute-start | bytes 9437192 | tf_op jit(solution)/shard_map/ppermute | solution.py:28
  140.8 1.3 collective-permute-start.2
  142.1 2.7 copy.24
  152.1 1.4 fusion.82
  153.5 1.4 fusion.85
  154.9 109.3 %collective-permute-done.3 = f32[2,8,24,2048]{3,2,1,0:T(8,128)} collective-permute-done((f32[2,8,24,2048]{3,2,1,0:T(8,128)}, f32[2,8,24,2048]{3,2,1,0:T(8,128)}, u32[]{:S(2)}, u32[]{:S(2)}) %collective-permute-start.3) | collective-permute-done | bytes 3145760 | tf_op jit(solution)/shard_map/ppermute | solution.py:28
  264.2 3.0 collective-permute-done.2
  267.2 3.9 %add_add_fusion = f32[2,8,24,2048]{3,2,1,0:T(8,128)S(1)} fusion(f32[2,8,24,2048]{3,2,1,0:T(8,128)} %collective-permute-done.3, f32[2,8,24,2048]{3,2,1,0:T(8,128)S(1)} %bitcast.113, f32[2,8,24,2048]{3,2,1,0:T(8,128)} %collective-permute-done.2), kind=kLoop, calls=%fused_computation.3 | loop fusion | flops 1572864 | bytes 12582912 | tf_op jit(solution)/shard_map/add | solution.py:172
  271.1 1.3 constant_dynamic-slice_fusion
  273.4 1.2 fusion.88
  274.7 1.3 fusion.91
  275.9 1.3 fusion.94
  279.7 1.2 fusion.103
  281.0 2.7 copy.28
  283.7 2.5 copy.29
  286.2 1.6 add_convert_fusion
  288.7 59.6 %reduce-scatter.2.cloned.1.call-done = f32[384,1024]{0,1:T(8,128)} async-done(((f32[3072,1024]{0,1:T(8,128)}), f32[384,1024]{0,1:T(8,128)}) %reduce-scatter.2.cloned.1.call-update) | async-done | bytes 1572880 | tf_op jit(solution)/shard_map/reduce_scatter | solution.py:179
  348.3 3.0 copy.27
  (330 shorter events, 50.6 us)
Async XLA Ops:
  7.2 23.6 %copy-start.37 = (bf16[256,1024]{1,0:T(8,128)(2,1)S(1)}, bf16[256,1024]{1,0:T(8,128)(2,1)}, u32[]{:S(2)}) copy-start(bf16[256,1024]{1,0:T(8,128)(2,1)} %param.14) | copy-start | bytes 1572868
  7.2 23.6 %copy-start.34 = (bf16[2,4,24,1024]{3,2,1,0:T(8,128)(2,1)S(1)}, bf16[2,4,24,1024]{3,2,1,0:T(8,128)(2,1)}, u32[]{:S(2)}) copy-start(bf16[2,4,24,1024]{3,2,1,0:T(8,128)(2,1)} %param.9) | copy-start | bytes 1179652
  7.2 15.5 %all-gather.3.cloned.1.call-start = ((), (), s32[]{:S(2)}) async-start(), calls=%async_computation.1 | async-start | bytes 2359296 | tf_op jit(solution)/shard_map/all_gather | solution.py:117
  9.4 38.8 %all-gather.5.cloned.1.call-start = ((), (), s32[]{:S(2)}) async-start(), calls=%async_computation.2 | async-start | bytes 1769472 | tf_op jit(solution)/shard_map/all_gather | solution.py:114
  10.1 270.9 %all-reduce.3.cloned.1.call-start = ((), (), s32[]{:S(2)}) async-start(), calls=%async_computation.4 | async-start | bytes 4194304 | tf_op jit(solution)/shard_map/psum | solution.py:178
  22.7 39.3 %collective-permute-start.1 = (bf16[2,8,24,2048]{3,2,1,0:T(8,128)(2,1)}, bf16[2,8,24,2048]{3,2,1,0:T(8,128)(2,1)}, u32[]{:S(2)}, u32[]{:S(2)}) collective-permute-start(bf16[2,8,24,2048]{3,2,1,0:T(8,128)(2,1)} %all-gather.3.cloned.1.call-done), channel_id=1, source_target_pairs={{4,0},{8,4},{12,8},{5,1},{9,5},{13,9},{6,2},{10,6},{14,10},{7,3},{... | collective-permute-start | bytes 4718600 | tf_op jit(solution)/shard_map/ppermute | solution.py:20
  24.0 39.2 %collective-permute-start = (bf16[2,8,24,2048]{3,2,1,0:T(8,128)(2,1)}, bf16[2,8,24,2048]{3,2,1,0:T(8,128)(2,1)}, u32[]{:S(2)}, u32[]{:S(2)}) collective-permute-start(bf16[2,8,24,2048]{3,2,1,0:T(8,128)(2,1)} %all-gather.3.cloned.1.call-done), channel_id=1, source_target_pairs={{0,4},{4,8},{8,12},{1,5},{5,9},{9,13},{2,6},{6,10},{10,14},{3,7},{... | collective-permute-start | bytes 4718600 | tf_op jit(solution)/shard_map/ppermute | solution.py:17
  30.4 37.2 %copy-start.63 = (s32[1152]{0:T(1024)}, s32[1152]{0:T(1024)S(1)}, u32[]{:S(2)}) copy-start(s32[1152]{0:T(1024)S(1)} %fusion.292) | copy-start | bytes 13828
  30.8 36.8 %copy-start.88 = (s32[192]{0:T(256)}, s32[192]{0:T(256)S(1)}, u32[]{:S(2)}) copy-start(s32[192]{0:T(256)S(1)} %get-tuple-element.26) | copy-start | bytes 2308
  30.8 36.8 %copy-start.90 = (s32[192]{0:T(256)}, s32[192]{0:T(256)S(1)}, u32[]{:S(2)}) copy-start(s32[192]{0:T(256)S(1)} %get-tuple-element.27) | copy-start | bytes 2308
  30.8 36.8 %copy-start.92 = (s32[192]{0:T(256)}, s32[192]{0:T(256)S(1)}, u32[]{:S(2)}) copy-start(s32[192]{0:T(256)S(1)} %get-tuple-element.28) | copy-start | bytes 2308
  30.8 36.8 %copy-start.94 = (s32[192]{0:T(256)}, s32[192]{0:T(256)S(1)}, u32[]{:S(2)}) copy-start(s32[192]{0:T(256)S(1)} %get-tuple-element.29) | copy-start | bytes 2308
  30.8 36.8 %copy-start.96 = (s32[192]{0:T(256)}, s32[192]{0:T(256)S(1)}, u32[]{:S(2)}) copy-start(s32[192]{0:T(256)S(1)} %get-tuple-element.30) | copy-start | bytes 2308
  30.9 36.8 %copy-start.98 = (s32[192]{0:T(256)}, s32[192]{0:T(256)S(1)}, u32[]{:S(2)}) copy-start(s32[192]{0:T(256)S(1)} %get-tuple-element.31) | copy-start | bytes 2308
  36.6 26.6 %copy-start.39 = (bf16[2,8,24,2048]{3,2,1,0:T(8,128)(2,1)S(1)}, bf16[2,8,24,2048]{3,2,1,0:T(8,128)(2,1)}, u32[]{:S(2)}) copy-start(bf16[2,8,24,2048]{3,2,1,0:T(8,128)(2,1)} %all-gather.3.cloned.1.call-done) | copy-start | bytes 4718596
  52.8 33.7 %copy-start.10 = (bf16[192,1024]{1,0:T(8,128)(2,1)}, bf16[192,1024]{1,0:T(8,128)(2,1)S(1)}, u32[]{:S(2)}) copy-start(bf16[192,1024]{1,0:T(8,128)(2,1)S(1)} %convolution_convert_fusion) | copy-start | bytes 1179652
  65.5 16.4 %copy-start = (bf16[6,8,24,2048]{3,2,1,0:T(8,128)(2,1)}, bf16[6,8,24,2048]{3,2,1,0:T(8,128)(2,1)S(1)}, u32[]{:S(2)}) copy-start(bf16[6,8,24,2048]{3,2,1,0:T(8,128)(2,1)S(1)} %pad_maximum_fusion) | copy-start | bytes 14155780
  66.2 15.7 %copy-start.8 = (f32[192,1152]{1,0:T(8,128)}, f32[192,1152]{1,0:T(8,128)S(1)}, u32[]{:S(2)}) copy-start(f32[192,1152]{1,0:T(8,128)S(1)} %get-tuple-element.40) | copy-start | bytes 2654212
  71.4 8.6 %copy-start.1 = (f32[192,1152]{1,0:T(8,128)}, f32[192,1152]{1,0:T(8,128)S(1)}, u32[]{:S(2)}) copy-start(f32[192,1152]{1,0:T(8,128)S(1)} %get-tuple-element.52) | copy-start | bytes 2654212
  72.1 8.2 %copy-start.3 = (f32[192,1152]{1,0:T(8,128)}, f32[192,1152]{1,0:T(8,128)S(1)}, u32[]{:S(2)}) copy-start(f32[192,1152]{1,0:T(8,128)S(1)} %get-tuple-element.48) | copy-start | bytes 2654212
  72.9 13.0 %copy-start.5 = (f32[192,1152]{1,0:T(8,128)}, f32[192,1152]{1,0:T(8,128)S(1)}, u32[]{:S(2)}) copy-start(f32[192,1152]{1,0:T(8,128)S(1)} %get-tuple-element.44) | copy-start | bytes 2654212
  74.0 12.5 %copy-start.61 = (f32[192]{0:T(256)}, f32[192]{0:T(256)S(1)}, u32[]{:S(2)}) copy-start(f32[192]{0:T(256)S(1)} %log_add_fusion) | copy-start | bytes 2308
  77.3 7.9 %copy-start.55 = (f32[192]{0:T(256)}, f32[192]{0:T(256)S(1)}, u32[]{:S(2)}) copy-start(f32[192]{0:T(256)S(1)} %log_add_fusion.5) | copy-start | bytes 2308
  81.9 11.9 %copy-start.54 = (bf16[192,1024]{1,0:T(8,128)(2,1)}, bf16[192,1024]{1,0:T(8,128)(2,1)S(1)}, u32[]{:S(2)}) copy-start(bf16[192,1024]{1,0:T(8,128)(2,1)S(1)} %get-tuple-element.84) | copy-start | bytes 1179652
  82.9 10.9 %copy-start.66 = (f32[192]{0:T(256)}, f32[192]{0:T(256)S(1)}, u32[]{:S(2)}) copy-start(f32[192]{0:T(256)S(1)} %get-tuple-element.18) | copy-start | bytes 2308
  82.9 10.9 %copy-start.68 = (f32[192]{0:T(256)}, f32[192]{0:T(256)S(1)}, u32[]{:S(2)}) copy-start(f32[192]{0:T(256)S(1)} %get-tuple-element.25) | copy-start | bytes 2308
  82.9 10.9 %copy-start.70 = (f32[192]{0:T(256)}, f32[192]{0:T(256)S(1)}, u32[]{:S(2)}) copy-start(f32[192]{0:T(256)S(1)} %get-tuple-element.24) | copy-start | bytes 2308
  82.9 10.9 %copy-start.72 = (f32[192]{0:T(256)}, f32[192]{0:T(256)S(1)}, u32[]{:S(2)}) copy-start(f32[192]{0:T(256)S(1)} %get-tuple-element.23) | copy-start | bytes 2308
  82.9 10.9 %copy-start.74 = (f32[192]{0:T(256)}, f32[192]{0:T(256)S(1)}, u32[]{:S(2)}) copy-start(f32[192]{0:T(256)S(1)} %get-tuple-element.22) | copy-start | bytes 2308
  83.0 10.9 %copy-start.76 = (f32[192]{0:T(256)}, f32[192]{0:T(256)S(1)}, u32[]{:S(2)}) copy-start(f32[192]{0:T(256)S(1)} %get-tuple-element.21) | copy-start | bytes 2308
  83.0 10.9 %copy-start.78 = (f32[192]{0:T(256)}, f32[192]{0:T(256)S(1)}, u32[]{:S(2)}) copy-start(f32[192]{0:T(256)S(1)} %get-tuple-element.20) | copy-start | bytes 2308
  83.0 10.9 %copy-start.79 = (f32[192]{0:T(256)}, f32[192]{0:T(256)S(1)}, u32[]{:S(2)}) copy-start(f32[192]{0:T(256)S(1)} %get-tuple-element.19) | copy-start | bytes 2308
  83.2 10.7 %copy-start.41 = (bf16[192,256]{1,0:T(8,128)(2,1)}, bf16[192,256]{1,0:T(8,128)(2,1)S(1)}, u32[]{:S(2)}) copy-start(bf16[192,256]{1,0:T(8,128)(2,1)S(1)} %fusion.63) | copy-start | bytes 294916
  84.2 7.9 %copy-start.51 = (bf16[192,256]{1,0:T(8,128)(2,1)}, bf16[192,256]{1,0:T(8,128)(2,1)S(1)}, u32[]{:S(2)}) copy-start(bf16[192,256]{1,0:T(8,128)(2,1)S(1)} %fusion.60) | copy-start | bytes 294916
  84.4 8.5 %copy-start.52 = (bf16[192,256]{1,0:T(8,128)(2,1)}, bf16[192,256]{1,0:T(8,128)(2,1)S(1)}, u32[]{:S(2)}) copy-start(bf16[192,256]{1,0:T(8,128)(2,1)S(1)} %fusion.61) | copy-start | bytes 294916
  84.8 9.1 %copy-start.53 = (bf16[192,256]{1,0:T(8,128)(2,1)}, bf16[192,256]{1,0:T(8,128)(2,1)S(1)}, u32[]{:S(2)}) copy-start(bf16[192,256]{1,0:T(8,128)(2,1)S(1)} %fusion.62) | copy-start | bytes 294916
  94.8 253.5 %reduce-scatter.2.cloned.1.call-start = ((), (), s32[]{:S(2)}) async-start(), calls=%async_computation.3 | async-start | bytes 14155776 | tf_op jit(solution)/shard_map/reduce_scatter | solution.py:179
  104.1 7.8 %copy-start.75 = (f32[192]{0:T(256)S(1)}, f32[192]{0:T(256)}, u32[]{:S(2)}) copy-start(f32[192]{0:T(256)} %copy-done.74) | copy-start | bytes 2308
  134.6 13.5 %copy-start.50 = (bf16[192,256]{1,0:T(8,128)(2,1)S(1)}, bf16[192,256]{1,0:T(8,128)(2,1)}, u32[]{:S(2)}) copy-start(bf16[192,256]{1,0:T(8,128)(2,1)} %copy-done.49) | copy-start | bytes 294916
  134.6 14.5 %copy-start.48 = (bf16[192,256]{1,0:T(8,128)(2,1)S(1)}, bf16[192,256]{1,0:T(8,128)(2,1)}, u32[]{:S(2)}) copy-start(bf16[192,256]{1,0:T(8,128)(2,1)} %copy-done.47) | copy-start | bytes 294916
  134.6 15.5 %copy-start.46 = (bf16[192,256]{1,0:T(8,128)(2,1)S(1)}, bf16[192,256]{1,0:T(8,128)(2,1)}, u32[]{:S(2)}) copy-start(bf16[192,256]{1,0:T(8,128)(2,1)} %copy-done.45) | copy-start | bytes 294916
  134.6 16.5 %copy-start.44 = (bf16[192,256]{1,0:T(8,128)(2,1)S(1)}, bf16[192,256]{1,0:T(8,128)(2,1)}, u32[]{:S(2)}) copy-start(bf16[192,256]{1,0:T(8,128)(2,1)} %copy-done.43) | copy-start | bytes 294916
  134.6 129.6 %collective-permute-start.3 = (f32[2,8,24,2048]{3,2,1,0:T(8,128)}, f32[2,8,24,2048]{3,2,1,0:T(8,128)}, u32[]{:S(2)}, u32[]{:S(2)}) collective-permute-start(f32[2,8,24,2048]{3,2,1,0:T(8,128)} %bitcast.147), channel_id=1, source_target_pairs={{0,4},{4,8},{8,12},{1,5},{5,9},{9,13},{2,6},{6,10},{10,14},{3,7},{... | collective-permute-start | bytes 9437192 | tf_op jit(solution)/shard_map/ppermute | solution.py:28
  140.8 126.4 %collective-permute-start.2 = (f32[2,8,24,2048]{3,2,1,0:T(8,128)}, f32[2,8,24,2048]{3,2,1,0:T(8,128)}, u32[]{:S(2)}, u32[]{:S(2)}) collective-permute-start(f32[2,8,24,2048]{3,2,1,0:T(8,128)} %bitcast.146), channel_id=1, source_target_pairs={{4,0},{8,4},{12,8},{5,1},{9,5},{13,9},{6,2},{10,6},{14,10},{7,3},{... | collective-permute-start | bytes 9437192 | tf_op jit(solution)/shard_map/ppermute | solution.py:28
  144.8 122.5 %copy-start.7 = (f32[384,2048]{1,0:T(8,128)S(1)}, f32[384,2048]{1,0:T(8,128)}, u32[]{:S(2)}) copy-start(f32[384,2048]{1,0:T(8,128)} %copy.24) | copy-start | bytes 9437188
  271.1 8.6 %copy-start.21 = (bf16[192,1152]{1,0:T(8,128)(2,1)S(1)}, bf16[192,1152]{1,0:T(8,128)(2,1)}, u32[]{:S(2)}) copy-start(bf16[192,1152]{1,0:T(8,128)(2,1)} %copy-done.20) | copy-start | bytes 1327108
  272.4 13.8 %collective-permute-start.4 = (f32[2,4,24,2048]{3,2,1,0:T(8,128)}, f32[2,4,24,2048]{3,2,1,0:T(8,128)}, u32[]{:S(2)}, u32[]{:S(2)}) collective-permute-start(f32[2,4,24,2048]{3,2,1,0:T(8,128)} %constant_dynamic-slice_fusion), channel_id=1, source_target_pairs={{0,1},{1,0},{2,3},{3,2},{4,5},{5,4},{6,7},{7,6},{8,9},{9,8},{10,11... | collective-permute-start | bytes 4718600 | tf_op jit(solution)/shard_map/ppermute | solution.py:38
  281.0 7.8 %copy-start.65 = (bf16[192,1024]{1,0:T(8,128)(2,1)}, bf16[192,1024]{1,0:T(8,128)(2,1)S(1)}, u32[]{:S(2)}) copy-start(bf16[192,1024]{1,0:T(8,128)(2,1)S(1)} %fusion.103) | copy-start | bytes 1179652
  (61 other events, 271.5 us)
Sparse Core Ops, SparseCore 0:
  10.1 12.4 all-gather.2
  24.2 23.9 all-gather.4
  94.9 81.0 all-reduce.2
  178.2 170.0 reduce-scatter.1
where the time goes:
time: 360 us; the launch traced here: 358 us
  waiting for transfers between devices  195 us (54%)
  matrix products  86.9 us (24%)
  local copies, waits for them, and re-layouts  29.5 us (8%)
  between operations  16.4 us (5%)
  starting transfers between devices  15.4 us (4%)
  other arithmetic  14.6 us (4%)
    ppermute x2, waiting for transfers between devices, from_behind(): return lax.ppermute(block, axis, route)  112 us
    reduce_scatter x1, waiting for transfers between devices, per_device(): lax.psum_scatter(lax.dot_general(grad_full, attn_all, (((0,), (0,)), ((),...  59.6 us
    dot_general x8, matrix products, query_side(): jnp.einsum('qd,kd->qk', query_h, text_key_h, preferred_element_type=jnp.f...  14.9 us
    unnamed x204, local copies, waits for them, and re-layouts  11.7 us
    all_gather x1, waiting for transfers between devices, per_device(): lax.all_gather(out_grad.reshape(row_count, -1), 'head', axis=1, tiled=True)  11.6 us
    dot_general x8, matrix products, query_side(): jnp.einsum('qd,kd->qk', grad_h, value_h, preferred_element_type=jnp.float32)  11 us
    dot_general x8, matrix products, query_side(): jnp.dot(ds_w, key_h, preferred_element_type=jnp.float32)  10.2 us
    ppermute x1, waiting for transfers between devices, with_halo(): lax.ppermute(lax.slice_in_dim(block, 0, width, axis=dim), axis, backward)  9.23 us
  transfers between devices with their start and end apart: 9, of which 7 were waited for; matrix products, arithmetic and copies ran while one was open for 26% of the time, Pallas kernels for 0%

commit v1 on v0

v1 whole, which is shorter than its diff:
```python
import functools

import jax
import jax.numpy as jnp
from jax import lax
from jax.experimental import pallas as pl
from jax.experimental.pallas import tpu as pltpu
from jax.sharding import PartitionSpec as P

HDIM = 128
TH = 2
TW = 8
WIN = 3

F32 = jnp.float32
BF16 = jnp.bfloat16


def contract(a, b, dims):
    return lax.dot_general(a, b, (dims, ((), ())), preferred_element_type=F32)


def head_kernel(bias_ref, q_ref, k_ref, v_ref, tk_ref, tv_ref, do_ref,
                dq_ref, o_ref, dk_ref, dv_ref, dtk_ref, dtv_ref):
    scale = HDIM ** -0.5
    ext = k_ref.shape[0]
    q, do, k, v, tk, tv = (r[...] for r in (q_ref, do_ref, k_ref, v_ref, tk_ref, tv_ref))
    s_w = contract(q, k, ((1,), (1,))) * scale + bias_ref[:, :ext]
    s_t = contract(q, tk, ((1,), (1,))) * scale + bias_ref[:, ext:]
    top = jnp.maximum(jnp.max(s_w, axis=1, keepdims=True), jnp.max(s_t, axis=1, keepdims=True))
    e_w = jnp.exp(s_w - top)
    e_t = jnp.exp(s_t - top)
    total = jnp.sum(e_w, axis=1, keepdims=True) + jnp.sum(e_t, axis=1, keepdims=True)
    inv = 1.0 / total
    p_w = e_w * inv
    p_t = e_t * inv
    pb_w = p_w.astype(BF16)
    pb_t = p_t.astype(BF16)
    o = (contract(pb_w, v, ((1,), (0,))) + contract(pb_t, tv, ((1,), (0,)))).astype(BF16)
    o_ref[...] = o
    delta = jnp.sum(do.astype(F32) * o.astype(F32), axis=1, keepdims=True)
    ds_w = (p_w * (contract(do, v, ((1,), (1,))) - delta)).astype(BF16)
    ds_t = (p_t * (contract(do, tv, ((1,), (1,))) - delta)).astype(BF16)
    dq = contract(ds_w, k, ((1,), (0,))) + contract(ds_t, tk, ((1,), (0,)))
    dq_ref[...] = (dq * scale).astype(BF16)
    dk_ref[...] = (contract(ds_w, q, ((0,), (0,))) * scale).astype(BF16)
    dv_ref[...] = contract(pb_w, do, ((0,), (0,))).astype(BF16)
    dtk_ref[...] = contract(ds_t, q, ((0,), (0,))) * scale
    dtv_ref[...] = contract(pb_t, do, ((0,), (0,)))


def attention(bias, q, k, v, tk, tv, do):
    rows, cols = q.shape
    ext = k.shape[0]
    txt = tk.shape[0]
    heads = cols // HDIM

    def per_head(n):
        return pl.BlockSpec((n, HDIM), lambda h: (0, h))

    return pl.pallas_call(
        head_kernel,
        grid=(heads,),
        in_specs=[pl.BlockSpec(bias.shape, lambda h: (0, 0)), per_head(rows), per_head(ext), per_head(ext),
                  per_head(txt), per_head(txt), per_head(rows)],
        out_specs=[per_head(rows), per_head(rows), per_head(ext), per_head(ext), per_head(txt), per_head(txt)],
        out_shape=[
            jax.ShapeDtypeStruct((rows, cols), BF16),
            jax.ShapeDtypeStruct((rows, cols), BF16),
            jax.ShapeDtypeStruct((ext, cols), BF16),
            jax.ShapeDtypeStruct((ext, cols), BF16),
            jax.ShapeDtypeStruct((txt, cols), F32),
            jax.ShapeDtypeStruct((txt, cols), F32),
        ],
        compiler_params=pltpu.CompilerParams(vmem_limit_bytes=48 * 1024 * 1024),
        name="heads",
    )(bias, q, k, v, tk, tv, do)


def make_bias(window_start, text_count, frames, height, col_count, full_h, txt):
    frame_first = lax.axis_index("seq") * frames
    row_first = lax.axis_index("hgt") * height
    halves = full_h // height
    rows = frames * height * col_count
    tiles_h, tiles_w = full_h // TH, col_count // TW
    own = jnp.arange(rows, dtype=jnp.int32)
    starts = lax.dynamic_slice_in_dim(window_start, frame_first, frames, 0)
    starts = lax.dynamic_slice_in_dim(starts, lax.axis_index("hgt") * (height // TH), height // TH, 1)
    starts = jnp.repeat(jnp.repeat(starts, TH, axis=1), TW, axis=2).reshape(rows, 3)
    key = jnp.arange(3 * halves * rows, dtype=jnp.int32)
    block = key // rows
    inner = key % rows
    kf = frame_first + (block // halves - 1) * frames + inner // (height * col_count)
    kr = ((block % halves) * height + inner // col_count % height) // TH
    kc = inner % col_count // TW
    ok = True
    for n, pos in enumerate((kf, kr, kc)):
        low = starts[:, n:n + 1]
        ok = ok & (pos[None] >= low) & (pos[None] < low + WIN)
    text_ok = jnp.broadcast_to((jnp.arange(txt, dtype=jnp.int32) < text_count[0])[None], (rows, txt))
    ok = jnp.concatenate([ok, text_ok], axis=1)
    return jnp.where(ok, F32(0), F32(-jnp.inf))


def per_device(
    queries, key_rows, value_rows, out_grad, w_out, text_keys, text_values, text_count, window_start
):
    frames, height, col_count, columns = queries.shape
    rows = frames * height * col_count
    halves = lax.axis_size("hgt")
    nz = lax.axis_size("seq")
    txt = text_keys.shape[0]
    up = [(i, i + 1) for i in range(nz - 1)]
    down = [(i + 1, i) for i in range(nz - 1)]
    grad_full = lax.all_gather(out_grad.reshape(rows, -1), "head", axis=1, tiled=True)

    def halo(x):
        x = x.reshape(rows, columns)
        slabs = jnp.stack([lax.ppermute(x, "seq", up), x, lax.ppermute(x, "seq", down)])
        return lax.all_gather(slabs, "hgt", axis=1).reshape(3 * halves * rows, columns)

    k_ext = halo(key_rows)
    v_ext = halo(value_rows)
    bias = make_bias(window_start, text_count, frames, height, col_count, height * halves, txt)
    grad_o = jnp.dot(grad_full, w_out, preferred_element_type=F32).astype(BF16)
    og = lax.all_to_all(grad_full, ("seq", "hgt"), split_axis=1, concat_axis=0, tiled=True)
    dq, o, dk, dv, dtk, dtv = attention(
        bias, queries.reshape(rows, columns), k_ext, v_ext, text_keys, text_values, grad_o
    )
    o_all = lax.all_gather(o, ("seq", "hgt"), axis=0, tiled=True)
    me = lax.axis_index("hgt")

    def back(part):
        part = part.reshape(3, halves, rows, columns)
        mine = lax.dynamic_index_in_dim(part, me, 1, keepdims=False)
        other = lax.dynamic_index_in_dim(part, 1 - me, 1, keepdims=False)
        got = lax.ppermute(other, "hgt", [(0, 1), (1, 0)])
        mine = mine.astype(F32) + got.astype(F32)
        low = lax.ppermute(mine[0].astype(BF16), "seq", down)
        high = lax.ppermute(mine[2].astype(BF16), "seq", up)
        mine = mine[1] + low.astype(F32) + high.astype(F32)
        return mine.astype(BF16).reshape(queries.shape)

    grad_key = back(dk)
    grad_value = back(dv)
    grad_text_key, grad_text_value = lax.psum((dtk, dtv), ("seq", "hgt"))
    grad_w_out = contract(og, o_all, ((0,), (0,)))
    return (dq.reshape(queries.shape), grad_key, grad_value, grad_w_out, grad_text_key, grad_text_value)


def solution(mesh):
    tok = P(("parts", "seq"), "hgt", None, "head")
    return jax.shard_map(
        per_device,
        mesh=mesh,
        in_specs=(tok, tok, tok, tok, P(None, "head"), P("parts", "head"), P("parts", "head"),
                  P("parts"), P("parts", None, None, None)),
        out_specs=(tok, tok, tok, P(("parts", "seq", "hgt"), "head"), P("parts", "head"), P("parts", "head")),
        check_vma=False,
    )
```

time: 360 us -> 223 us (0.62)
  matrix products: 86.9 us -> 8.71 us
  waiting for transfers between devices: 195 us -> 128 us
  local copies, waits for them, and re-layouts: 29.5 us -> 11.9 us
  Pallas kernels: 0 us -> 15.5 us
  starting transfers between devices: 15.4 us -> 29.7 us
    dot_general x98 -> x2, matrix products: 86.9 us -> 8.71 us  [the longest x1 4.63 us: per_device(): grad_o = jnp.dot(grad_full, w_out, preferred_element_type=F32).astype(BF16)]
    ppermute x5 -> x10, waiting for transfers between devices: 123 us -> 62.7 us  [the longest x2 41.2 us: back(): low = lax.ppermute(mine[0].astype(BF16), 'seq', down)]
    reduce_scatter x1 -> x0, waiting for transfers between devices: 59.6 us -> none  [per_device(): lax.psum_scatter(lax.dot_general(grad_full, attn_all, (((0,), (0,)), ((),...]
    psum x1, waiting for transfers between devices: 0.02 us -> 54.3 us  [per_device(): grad_text_key, grad_text_value = lax.psum((dtk, dtv), ('seq', 'hgt'))]
    pallas_call x0 -> x1, Pallas kernels: none -> 15.5 us  [attention(): pl.pallas_call(head_kernel, grid=(heads,), in_specs=[pl.BlockSpec(bias.sh...]
    slice x5 -> x0, local copies, waits for them, and re-layouts: 14.2 us -> none  [the longest x2 6.98 us: per_device(): from_upper = from_behind(contrib[:frames], 'seq', -1)]
    ppermute x5 -> x10, starting transfers between devices: 15.2 us -> 24.7 us  [the longest x2 10.6 us: back(): high = lax.ppermute(mine[2].astype(BF16), 'seq', up)]
    another operation x1 -> x4, other arithmetic: 1.58 us -> 8.78 us
  transfers between devices with their start and end apart: 9 -> 16, of which waited for: 7 -> 8; matrix products, arithmetic and copies ran while one was open for 26% -> 13% of each run, Pallas kernels for 0% -> 0%
where the time goes in v1:
time: 223 us; the launch traced here: 222 us
  waiting for transfers between devices  128 us (57%)
  starting transfers between devices  29.7 us (13%)
  Pallas kernels  15.5 us (7%)
  between operations  14.7 us (7%)
  other arithmetic  13.8 us (6%)
  local copies, waits for them, and re-layouts  11.9 us (5%)
  matrix products  8.71 us (4%)
    psum x1, waiting for transfers between devices, per_device(): grad_text_key, grad_text_value = lax.psum((dtk, dtv), ('seq', 'hgt'))  54.3 us
    ppermute x2, waiting for transfers between devices, back(): low = lax.ppermute(mine[0].astype(BF16), 'seq', down)  41.2 us
    pallas_call x1, Pallas kernels, attention(): pl.pallas_call(head_kernel, grid=(heads,), in_specs=[pl.BlockSpec(bias.sh...  15.5 us
    ppermute x2, waiting for transfers between devices, halo(): lax.ppermute(x, 'seq', up)  13.3 us
    ppermute x2, starting transfers between devices, back(): high = lax.ppermute(mine[2].astype(BF16), 'seq', up)  10.6 us
    all_gather x2, waiting for transfers between devices, halo(): lax.all_gather(slabs, 'hgt', axis=1).reshape(3 * halves * rows, columns)  10.4 us
    ppermute x2, starting transfers between devices, halo(): lax.ppermute(x, 'seq', up)  8.42 us
    ppermute x2, waiting for transfers between devices, halo(): lax.ppermute(x, 'seq', down)  8.17 us
  transfers between devices with their start and end apart: 16, of which 8 were waited for; matrix products, arithmetic and copies ran while one was open for 13% of the time, Pallas kernels for 0%

profile of v1, /device:TPU:0, one launch (start us, length us, event | category | flops | bytes accessed | tf_op | source)
XLA Modules:
  0.0 222.5 jit_solution(17220047459413305369)
XLA Ops:
  7.2 0.7 all-gather.7.cloned.1.call-update
  8.0 5.0 %collective-permute-start = (bf16[192,1024]{1,0:T(8,128)(2,1)}, bf16[192,1024]{1,0:T(8,128)(2,1)S(1)}, u32[]{:S(2)}, u32[]{:S(2)}) collective-permute-start(bf16[192,1024]{1,0:T(8,128)(2,1)} %bitcast.86), channel_id=1, source_target_pairs={{0,4},{4,8},{8,12},{1,5},{5,9},{9,13},{2,6},{6,10},{10,14},{3,7},{... | collective-permute-start | bytes 1179656 | tf_op jit(solution)/shard_map/ppermute | solution.py:119
  12.9 1.3 collective-permute-start.1
  14.2 7.3 %collective-permute-done = bf16[192,1024]{1,0:T(8,128)(2,1)S(1)} collective-permute-done((bf16[192,1024]{1,0:T(8,128)(2,1)}, bf16[192,1024]{1,0:T(8,128)(2,1)S(1)}, u32[]{:S(2)}, u32[]{:S(2)}) %collective-permute-start) | collective-permute-done | bytes 393248 | tf_op jit(solution)/shard_map/ppermute | solution.py:119
  21.6 4.0 %collective-permute-done.1 = bf16[192,1024]{1,0:T(8,128)(2,1)S(1)} collective-permute-done((bf16[192,1024]{1,0:T(8,128)(2,1)}, bf16[192,1024]{1,0:T(8,128)(2,1)S(1)}, u32[]{:S(2)}, u32[]{:S(2)}) %collective-permute-start.1) | collective-permute-done | bytes 393248 | tf_op jit(solution)/shard_map/ppermute | solution.py:119
  25.6 2.1 pad_maximum_fusion
  27.8 0.9 copy-done.8
  28.7 3.5 %collective-permute-start.2 = (bf16[192,1024]{1,0:T(8,128)(2,1)S(1)}, bf16[192,1024]{1,0:T(8,128)(2,1)S(1)}, u32[]{:S(2)}, u32[]{:S(2)}) collective-permute-start(bf16[192,1024]{1,0:T(8,128)(2,1)S(1)} %bitcast.89), channel_id=1, source_target_pairs={{0,4},{4,8},{8,12},{1,5},{5,9},{9,13},{2,6},{6,10},{10,14},{3,7},{... | collective-permute-start | bytes 1179656 | tf_op jit(solution)/shard_map/ppermute | solution.py:119
  32.2 1.3 collective-permute-start.3
  33.5 5.9 %collective-permute-done.2 = bf16[192,1024]{1,0:T(8,128)(2,1)S(1)} collective-permute-done((bf16[192,1024]{1,0:T(8,128)(2,1)S(1)}, bf16[192,1024]{1,0:T(8,128)(2,1)S(1)}, u32[]{:S(2)}, u32[]{:S(2)}) %collective-permute-start.2) | collective-permute-done | bytes 393248 | tf_op jit(solution)/shard_map/ppermute | solution.py:119
  39.5 4.1 %collective-permute-done.3 = bf16[192,1024]{1,0:T(8,128)(2,1)S(1)} collective-permute-done((bf16[192,1024]{1,0:T(8,128)(2,1)S(1)}, bf16[192,1024]{1,0:T(8,128)(2,1)S(1)}, u32[]{:S(2)}, u32[]{:S(2)}) %collective-permute-start.3) | collective-permute-done | bytes 393248 | tf_op jit(solution)/shard_map/ppermute | solution.py:119
  43.6 1.2 pad_maximum_fusion.1
  44.8 0.0 all-gather.9.cloned.1.call-start
  44.9 0.1 constant_dynamic-slice_fusion
  44.9 0.1 copy.25
  45.1 0.1 copy.26
  45.2 0.1 broadcast_in_dim.13
  45.3 0.1 reshape_reshape.3
  46.2 0.5 compare_and_fusion
  46.7 0.1 add_select_fusion.bias_ref
  46.9 4.6 %convolution_convert_fusion.do_ref = bf16[192,1024]{1,0:T(8,128)(2,1)S(1)} fusion(bf16[192,3072]{1,0:T(8,128)(2,1)} %all-gather.7.cloned.1.call-done, bf16[3072,1024]{1,0:T(8,128)(2,1)} %param.13), kind=kOutput, calls=%fused_computation.3 | convolution fusion | flops 1208156160 | bytes 7864320 | tf_op jit(solution)/shard_map/dot_general | solution.py:125
  51.6 10.4 %all-gather.13.cloned.1.call-done = bf16[3,384,1024]{2,1,0:T(8,128)(2,1)} async-done(((bf16[3,192,1024]{2,1,0:T(8,128)(2,1)}), bf16[3,384,1024]{2,1,0:T(8,128)(2,1)}) %all-gather.13.cloned.1.call-update) | async-done | bytes 2359312 | tf_op jit(solution)/shard_map/all_gather | solution.py:120
  61.9 15.5 %heads.1 = (bf16[192,1024]{1,0:T(8,128)(2,1)}, bf16[192,1024]{1,0:T(8,128)(2,1)}, bf16[1152,1024]{1,0:T(8,128)(2,1)}, bf16[1152,1024]{1,0:T(8,128)(2,1)}, f32[256,1024]{1,0:T(8,128)}, /*index=5*/f32[256,1024]{1,0:T(8,128)}) custom-call(f32[192,1408]{1,0:T(8,128)S(1)} %add_select_fusion.bias_ref, bf16[192,1024]{1,0:T(8,128)(2,1)S(1)} %bitcast.77, ...), custom_call_target="tpu_custom_call" | custom-call | tf_op jit(solution)/shard_map/heads/pallas_call | solution.py:61
  77.5 1.5 dynamic-slice_bitcast_fusion
  79.0 0.3 collective-permute-start.7
  79.3 0.2 copy-done.4
  79.5 1.1 dynamic-slice_bitcast_fusion.1
  80.6 0.2 collective-permute-start.4
  80.8 0.4 copy-done.6
  81.2 1.2 copy.31
  82.4 4.9 %all-to-all-start = ((bf16[192,8,384]{2,0,1:T(8,128)(2,1)}), bf16[192,8,384]{2,0,1:T(8,128)(2,1)}, u32[]{:S(2)}, u32[]{:S(2)}) async-start(bf16[192,8,384]{2,0,1:T(8,128)(2,1)} %bitcast.75), calls=%async_computation | async-start | bytes 2359296 | tf_op jit(solution)/shard_map/all_to_all | solution.py:126
  87.3 2.3 %fusion.37 = (bf16[3,192,1024]{2,1,0:T(8,128)(2,1)S(1)}, f32[3,192,1024]{2,1,0:T(8,128)S(1)}) fusion(bf16[3,192,1024]{2,1,0:T(8,128)(2,1)} %collective-permute-done.7, bf16[3,2,192,1024]{3,2,1,0:T(8,128)(2,1)} %bitcast.81, s32[]{:T(128)S(6)} %select_n.150), kind=kLoop, calls=%fused_computation.85 | loop fusion | flops 2359296 | bytes 5898244 | tf_op jit(solution)/shard_map/convert.3
  89.6 0.1 slice_bitcast_fusion.3
  89.7 1.3 collective-permute-start.8
  91.0 5.3 %collective-permute-start.9 = (bf16[192,1024]{1,0:T(8,128)(2,1)S(1)}, bf16[192,1024]{1,0:T(8,128)(2,1)}, u32[]{:S(2)}, u32[]{:S(2)}) collective-permute-start(bf16[192,1024]{1,0:T(8,128)(2,1)S(1)} %get-tuple-element.49), channel_id=1, source_target_pairs={{0,4},{4,8},{8,12},{1,5},{5,9},{9,13},{2,6},{6,10},{10,14},{3,7},{... | collective-permute-start | bytes 1179656 | tf_op jit(solution)/shard_map/ppermute | solution.py:140
  96.3 3.2 %fusion.38 = (bf16[3,192,1024]{2,1,0:T(8,128)(2,1)S(1)}, f32[3,192,1024]{2,1,0:T(8,128)}) fusion(bf16[3,192,1024]{2,1,0:T(8,128)(2,1)} %collective-permute-done.4, bf16[3,2,192,1024]{3,2,1,0:T(8,128)(2,1)S(1)} %bitcast.79, s32[]{:T(128)S(6)} %select_n.150), kind=kLoop, calls=%fused_computation.86 | loop fusion | flops 2359296 | bytes 5898244 | tf_op jit(solution)/shard_map/convert.5
  99.5 0.9 slice_bitcast_fusion.5
  100.4 1.3 collective-permute-start.5
  101.7 5.3 %collective-permute-start.6 = (bf16[192,1024]{1,0:T(8,128)(2,1)}, bf16[192,1024]{1,0:T(8,128)(2,1)}, u32[]{:S(2)}, u32[]{:S(2)}) collective-permute-start(bf16[192,1024]{1,0:T(8,128)(2,1)} %get-tuple-element.51), channel_id=1, source_target_pairs={{0,4},{4,8},{8,12},{1,5},{5,9},{9,13},{2,6},{6,10},{10,14},{3,7},{... | collective-permute-start | bytes 1179656 | tf_op jit(solution)/shard_map/ppermute | solution.py:140
  107.0 34.9 %collective-permute-done.8 = bf16[192,1024]{1,0:T(8,128)(2,1)} collective-permute-done((bf16[192,1024]{1,0:T(8,128)(2,1)S(1)}, bf16[192,1024]{1,0:T(8,128)(2,1)}, u32[]{:S(2)}, u32[]{:S(2)}) %collective-permute-start.8) | collective-permute-done | bytes 393248 | tf_op jit(solution)/shard_map/ppermute | solution.py:139
  141.9 2.0 fusion.2
  143.9 6.4 %collective-permute-done.5 = bf16[192,1024]{1,0:T(8,128)(2,1)} collective-permute-done((bf16[192,1024]{1,0:T(8,128)(2,1)}, bf16[192,1024]{1,0:T(8,128)(2,1)}, u32[]{:S(2)}, u32[]{:S(2)}) %collective-permute-start.5) | collective-permute-done | bytes 393248 | tf_op jit(solution)/shard_map/ppermute | solution.py:139
  150.3 2.3 %fusion.5 = bf16[192,1024]{1,0:T(8,128)(2,1)} fusion(f32[3,192,1024]{2,1,0:T(8,128)} %get-tuple-element.47, bf16[192,1024]{1,0:T(8,128)(2,1)} %collective-permute-done.6, bf16[192,1024]{1,0:T(8,128)(2,1)} %collective-permute-done.5), kind=kLoop, calls=%fused_computation.18 | loop fusion | flops 983040 | bytes 1966080 | tf_op jit(solution)/shard_map/convert_element_type | solution.py:142
  152.6 4.1 %convolution_bitcast_fusion = f32[384,1024]{0,1:T(8,128)S(1)} fusion(bf16[1536,1024]{1,0:T(8,128)(2,1)} %all-gather.9.cloned.1.call-done, bf16[1536,384]{1,0:T(8,128)(2,1)} %bitcast.36), kind=kOutput, calls=%fused_computation.2 | convolution fusion | flops 1207959552 | bytes 5898240 | tf_op jit(solution)/shard_map/dot_general | solution.py:20
  156.7 1.6 copy.28
  158.3 54.3 %all-reduce.3.cloned.1.call-done = (f32[256,1024]{1,0:T(8,128)}, f32[256,1024]{1,0:T(8,128)}) async-done(((f32[256,1024]{1,0:T(8,128)}, f32[256,1024]{1,0:T(8,128)}), (f32[256,1024]{1,0:T(8,128)}, f32[256,1024]{1,0:T(8,128)})) %all-reduce.3.cloned.1.call-update) | async-done | bytes 2097168 | tf_op jit(solution)/shard_map/psum | solution.py:146
  212.6 2.4 %copy.35 = f32[256,1024]{1,0:T(8,128)} copy(f32[256,1024]{1,0:T(8,128)} %get-tuple-element.64) | data formatting | bytes 2097152
  215.0 1.0 copy.36
  (37 shorter events, 0.4 us)
Async XLA Ops:
  7.2 37.7 %copy-start = (s32[8,4,3,3]{0,1,3,2:T(4,128)S(1)}, s32[8,4,3,3]{0,1,3,2:T(4,128)}, u32[]{:S(2)}) copy-start(s32[8,4,3,3]{0,1,3,2:T(4,128)} %param.17) | copy-start | bytes 3460
  7.2 39.7 %all-gather.7.cloned.1.call-start = ((), (), s32[]{:S(2)}) async-start(), calls=%async_computation.1 | async-start | bytes 1769472 | tf_op jit(solution)/shard_map/all_gather | solution.py:115
  7.9 43.6 %all-gather.11.cloned.1.call-start = ((), (), s32[]{:S(2)}) async-start(), calls=%async_computation.3 | async-start | bytes 3538944 | tf_op jit(solution)/shard_map/all_gather | solution.py:120
  8.0 13.6 %collective-permute-start = (bf16[192,1024]{1,0:T(8,128)(2,1)}, bf16[192,1024]{1,0:T(8,128)(2,1)S(1)}, u32[]{:S(2)}, u32[]{:S(2)}) collective-permute-start(bf16[192,1024]{1,0:T(8,128)(2,1)} %bitcast.86), channel_id=1, source_target_pairs={{0,4},{4,8},{8,12},{1,5},{5,9},{9,13},{2,6},{6,10},{10,14},{3,7},{... | collective-permute-start | bytes 1179656 | tf_op jit(solution)/shard_map/ppermute | solution.py:119
  12.9 12.7 %collective-permute-start.1 = (bf16[192,1024]{1,0:T(8,128)(2,1)}, bf16[192,1024]{1,0:T(8,128)(2,1)S(1)}, u32[]{:S(2)}, u32[]{:S(2)}) collective-permute-start(bf16[192,1024]{1,0:T(8,128)(2,1)} %bitcast.87), channel_id=1, source_target_pairs={{4,0},{8,4},{12,8},{5,1},{9,5},{13,9},{6,2},{10,6},{14,10},{7,3},{... | collective-permute-start | bytes 1179656 | tf_op jit(solution)/shard_map/ppermute | solution.py:119
  27.7 1.0 copy-start.8
  27.8 34.2 %all-gather.13.cloned.1.call-start = ((), (), s32[]{:S(2)}) async-start(), calls=%async_computation.4 | async-start | bytes 3538944 | tf_op jit(solution)/shard_map/all_gather | solution.py:120
  28.7 10.7 %collective-permute-start.2 = (bf16[192,1024]{1,0:T(8,128)(2,1)S(1)}, bf16[192,1024]{1,0:T(8,128)(2,1)S(1)}, u32[]{:S(2)}, u32[]{:S(2)}) collective-permute-start(bf16[192,1024]{1,0:T(8,128)(2,1)S(1)} %bitcast.89), channel_id=1, source_target_pairs={{0,4},{4,8},{8,12},{1,5},{5,9},{9,13},{2,6},{6,10},{10,14},{3,7},{... | collective-permute-start | bytes 1179656 | tf_op jit(solution)/shard_map/ppermute | solution.py:119
  32.2 11.4 %collective-permute-start.3 = (bf16[192,1024]{1,0:T(8,128)(2,1)S(1)}, bf16[192,1024]{1,0:T(8,128)(2,1)S(1)}, u32[]{:S(2)}, u32[]{:S(2)}) collective-permute-start(bf16[192,1024]{1,0:T(8,128)(2,1)S(1)} %bitcast.90), channel_id=1, source_target_pairs={{4,0},{8,4},{12,8},{5,1},{9,5},{13,9},{6,2},{10,6},{14,10},{7,3},{... | collective-permute-start | bytes 1179656 | tf_op jit(solution)/shard_map/ppermute | solution.py:119
  44.8 107.8 %all-gather.9.cloned.1.call-start = ((), (), s32[]{:S(2)}) async-start(), calls=%async_computation.2 | async-start | bytes 3538944 | tf_op jit(solution)/shard_map/all_gather | solution.py:130
  46.8 15.1 %copy-start.1 = (bf16[256,1024]{1,0:T(8,128)(2,1)S(1)}, bf16[256,1024]{1,0:T(8,128)(2,1)}, u32[]{:S(2)}) copy-start(bf16[256,1024]{1,0:T(8,128)(2,1)} %tk_ref.1) | copy-start | bytes 1572868
  46.8 15.1 %copy-start.2 = (bf16[256,1024]{1,0:T(8,128)(2,1)S(1)}, bf16[256,1024]{1,0:T(8,128)(2,1)}, u32[]{:S(2)}) copy-start(bf16[256,1024]{1,0:T(8,128)(2,1)} %tv_ref.1) | copy-start | bytes 1572868
  46.9 15.1 %copy-start.3 = (bf16[2,4,24,1024]{3,2,1,0:T(8,128)(2,1)S(1)}, bf16[2,4,24,1024]{3,2,1,0:T(8,128)(2,1)}, u32[]{:S(2)}) copy-start(bf16[2,4,24,1024]{3,2,1,0:T(8,128)(2,1)} %param.9) | copy-start | bytes 1179652
  77.5 2.0 copy-start.4
  79.0 8.3 %collective-permute-start.7 = (bf16[3,192,1024]{2,1,0:T(8,128)(2,1)S(1)}, bf16[3,192,1024]{2,1,0:T(8,128)(2,1)}, u32[]{:S(2)}, u32[]{:S(2)}) collective-permute-start(bf16[3,192,1024]{2,1,0:T(8,128)(2,1)S(1)} %dynamic-slice_bitcast_fusion), channel_id=1, source_target_pairs={{0,1},{1,0},{2,3},{3,2},{4,5},{5,4},{6,7},{7,6},{8,9},{9,8},{10,11... | collective-permute-start | bytes 3538952 | tf_op jit(solution)/shard_map/ppermute | solution.py:137
  79.5 1.7 copy-start.6
  80.6 15.7 %collective-permute-start.4 = (bf16[3,192,1024]{2,1,0:T(8,128)(2,1)}, bf16[3,192,1024]{2,1,0:T(8,128)(2,1)}, u32[]{:S(2)}, u32[]{:S(2)}) collective-permute-start(bf16[3,192,1024]{2,1,0:T(8,128)(2,1)} %dynamic-slice_bitcast_fusion.1), channel_id=1, source_target_pairs={{0,1},{1,0},{2,3},{3,2},{4,5},{5,4},{6,7},{7,6},{8,9},{9,8},{10,11... | collective-permute-start | bytes 3538952 | tf_op jit(solution)/shard_map/ppermute | solution.py:137
  82.4 70.2 %all-to-all-start = ((bf16[192,8,384]{2,0,1:T(8,128)(2,1)}), bf16[192,8,384]{2,0,1:T(8,128)(2,1)}, u32[]{:S(2)}, u32[]{:S(2)}) async-start(bf16[192,8,384]{2,0,1:T(8,128)(2,1)} %bitcast.75), calls=%async_computation | async-start | bytes 2359296 | tf_op jit(solution)/shard_map/all_to_all | solution.py:126
  87.2 125.3 %all-reduce.3.cloned.1.call-start = ((), (), s32[]{:S(2)}) async-start(), calls=%async_computation.5 | async-start | bytes 4194304 | tf_op jit(solution)/shard_map/psum | solution.py:146
  87.3 9.0 %copy-start.5 = (bf16[1152,1024]{1,0:T(8,128)(2,1)S(1)}, bf16[1152,1024]{1,0:T(8,128)(2,1)}, u32[]{:S(2)}) copy-start(bf16[1152,1024]{1,0:T(8,128)(2,1)} %get-tuple-element.13) | copy-start | bytes 7077892
  89.7 52.2 %collective-permute-start.8 = (bf16[192,1024]{1,0:T(8,128)(2,1)S(1)}, bf16[192,1024]{1,0:T(8,128)(2,1)}, u32[]{:S(2)}, u32[]{:S(2)}) collective-permute-start(bf16[192,1024]{1,0:T(8,128)(2,1)S(1)} %get-tuple-element.48), channel_id=1, source_target_pairs={{4,0},{8,4},{12,8},{5,1},{9,5},{13,9},{6,2},{10,6},{14,10},{7,3},{... | collective-permute-start | bytes 1179656 | tf_op jit(solution)/shard_map/ppermute | solution.py:139
  91.0 50.9 %collective-permute-start.9 = (bf16[192,1024]{1,0:T(8,128)(2,1)S(1)}, bf16[192,1024]{1,0:T(8,128)(2,1)}, u32[]{:S(2)}, u32[]{:S(2)}) collective-permute-start(bf16[192,1024]{1,0:T(8,128)(2,1)S(1)} %get-tuple-element.49), channel_id=1, source_target_pairs={{0,4},{4,8},{8,12},{1,5},{5,9},{9,13},{2,6},{6,10},{10,14},{3,7},{... | collective-permute-start | bytes 1179656 | tf_op jit(solution)/shard_map/ppermute | solution.py:140
  100.4 49.9 %collective-permute-start.5 = (bf16[192,1024]{1,0:T(8,128)(2,1)}, bf16[192,1024]{1,0:T(8,128)(2,1)}, u32[]{:S(2)}, u32[]{:S(2)}) collective-permute-start(bf16[192,1024]{1,0:T(8,128)(2,1)} %get-tuple-element.50), channel_id=1, source_target_pairs={{4,0},{8,4},{12,8},{5,1},{9,5},{13,9},{6,2},{10,6},{14,10},{7,3},{... | collective-permute-start | bytes 1179656 | tf_op jit(solution)/shard_map/ppermute | solution.py:139
  101.7 48.6 %collective-permute-start.6 = (bf16[192,1024]{1,0:T(8,128)(2,1)}, bf16[192,1024]{1,0:T(8,128)(2,1)}, u32[]{:S(2)}, u32[]{:S(2)}) collective-permute-start(bf16[192,1024]{1,0:T(8,128)(2,1)} %get-tuple-element.51), channel_id=1, source_target_pairs={{0,4},{4,8},{8,12},{1,5},{5,9},{9,13},{2,6},{6,10},{10,14},{3,7},{... | collective-permute-start | bytes 1179656 | tf_op jit(solution)/shard_map/ppermute | solution.py:140
  212.6 2.4 %copy-start.7 = (f32[256,1024]{1,0:T(8,128)S(1)}, f32[256,1024]{1,0:T(8,128)}, u32[]{:S(2)}) copy-start(f32[256,1024]{1,0:T(8,128)} %get-tuple-element.65) | copy-start | bytes 3145732
Sparse Core Ops, SparseCore 0:
  9.6 25.4 all-gather.6
  37.2 10.9 all-gather.10
  49.7 12.1 all-gather.12
  77.6 64.4 all-gather.8
  144.9 67.6 all-reduce.2

commit v2 on v1

v2 whole, which is shorter than its diff:
```python
import functools

import jax
import jax.numpy as jnp
import numpy as np
from jax import lax
from jax.experimental import pallas as pl
from jax.experimental.pallas import tpu as pltpu
from jax.sharding import PartitionSpec as P

HDIM = 128
TH = 2
TW = 8
WIN = 3

F32 = jnp.float32
BF16 = jnp.bfloat16
MESH = pl.DeviceIdType.MESH


def contract(a, b, dims):
    return lax.dot_general(a, b, (dims, ((), ())), preferred_element_type=F32)


def body(cfg, window, count, key_table, tile_table, q_in, k_in, v_in, og_in, w_in, tk_in, tv_in,
         dq_out, dk_out, dv_out, gw_out, dtk_out, dtv_out,
         q, tk, tv, w, do, bias, gfull, stage, a_all, k_ext, v_ext, dk_part, dv_part, k_got, v_got,
         k_sum, v_sum, k_mid, v_mid, k_ret, v_ret, o_all, t_part, t_got, t_sum, t_red, t_all,
         loc, og_s, og_r, kv_s, kv_r, kp_s, kp_r, a_s, a_r, pr_s, pr_r, rz_s, rz_r,
         o_s, o_r, of_s, of_r, tp_s, tp_r, ts_s, ts_r, tg_s, tg_r, tf_s, tf_r):
    nz, nx, rows, cols, groups, frames, height, width = cfg
    txt = tk_in.shape[0]
    slot = og_in.shape[1]
    chunk = stage.shape[2]
    share = txt // nz
    ext = 6 * rows
    heads = cols // HDIM
    per = heads // groups
    gcols = per * HDIM
    scale = HDIM ** -0.5
    y, z, x, c = (lax.axis_index(n) for n in ("parts", "seq", "head", "hgt"))
    partner = (y, z, x, 1 - c)
    up = (y, lax.rem(z + 1, nz), x, c)
    down = (y, lax.rem(z + nz - 1, nz), x, c)
    has_up = z < nz - 1
    has_down = z > 0

    def seq_peer(step):
        zt = lax.rem(z + step, nz)
        return zt, (y, zt, x, c)

    def copy(src, dst, s, r, dev):
        return pltpu.make_async_remote_copy(
            src_ref=src, dst_ref=dst, send_sem=s, recv_sem=r, device_id=dev, device_id_type=MESH)

    def got(dst, s, r):
        copy(dst, dst, s, r, partner).wait_recv()

    def row_block(n, size):
        return pl.ds(pl.multiple_of(n * size, 16), size)

    def key_rows(half, slab):
        return row_block(half * 3 + slab, rows)

    sent = []

    def send(when, make):
        if when is None:
            make().start()
        else:
            pl.when(when)(lambda: make().start())
        sent.append((when, make))

    locals_ = [
        pltpu.make_async_copy(w_in, w, loc.at[0]),
        pltpu.make_async_copy(q_in, q, loc.at[1]),
        pltpu.make_async_copy(tk_in, tk, loc.at[2]),
        pltpu.make_async_copy(tv_in, tv, loc.at[3]),
        pltpu.make_async_copy(k_in, k_ext.at[key_rows(c, 1)], loc.at[4]),
        pltpu.make_async_copy(v_in, v_ext.at[key_rows(c, 1)], loc.at[5]),
        pltpu.make_async_copy(og_in, gfull.at[x], loc.at[6]),
    ]
    locals_[6].start()
    for n in range(6):
        locals_[n].start()

    barrier = pltpu.get_barrier_semaphore()
    for step in range(nz):
        zt, dev = seq_peer(step)
        if step:
            pl.semaphore_signal(barrier, inc=1, device_id=dev, device_id_type=MESH)
        pl.semaphore_signal(barrier, inc=1, device_id=(y, zt, x, 1 - c), device_id_type=MESH)
    for step in range(1, nx):
        pl.semaphore_signal(barrier, inc=1, device_id=(y, z, lax.rem(x + step, nx), c), device_id_type=MESH)
    pl.semaphore_wait(barrier, 2 * nz - 1 + nx - 1)

    for step in range(1, nx):
        send(None, lambda step=step: copy(og_in, gfull.at[x], og_s.at[step], og_r.at[step],
                                          (y, z, lax.rem(x + step, nx), c)))
    for n, (src, dst) in enumerate(((k_in, k_ext), (v_in, v_ext))):
        send(has_up, lambda n=n, src=src, dst=dst: copy(
            src, dst.at[key_rows(c, 0)], kv_s.at[0, n], kv_r.at[0, n], up))
        send(has_down, lambda n=n, src=src, dst=dst: copy(
            src, dst.at[key_rows(c, 2)], kv_s.at[1, n], kv_r.at[1, n], down))
    for n, (src, dst) in enumerate(((k_in, k_ext), (v_in, v_ext))):
        send(None, lambda n=n, src=src, dst=dst: copy(
            src, dst.at[key_rows(c, 1)], kp_s.at[1, n], kp_r.at[1, n], partner))

    @pl.when(jnp.logical_not(has_down))
    def _():
        for ref in (k_ext, v_ext):
            for half in range(2):
                ref[pl.ds(half * 3 * rows, rows), :] = jnp.zeros((rows, cols), BF16)
        for ref in (k_ret, v_ret):
            ref[0] = jnp.zeros((rows, cols), BF16)

    @pl.when(jnp.logical_not(has_up))
    def _():
        for ref in (k_ext, v_ext):
            for half in range(2):
                ref[pl.ds((half * 3 + 2) * rows, rows), :] = jnp.zeros((rows, cols), BF16)
        for ref in (k_ret, v_ret):
            ref[1] = jnp.zeros((rows, cols), BF16)

    tile_id = tile_table[...]
    tiles_h, tiles_w = 2 * height // TH, width // TW
    ok = None
    for n in range(3):
        low = jnp.zeros((rows, 1), jnp.int32)
        t = 0
        for f in range(frames):
            for r in range(height // TH):
                for e in range(tiles_w):
                    at = (((z * frames + f) * tiles_h + c * (height // TH) + r) * tiles_w + e) * 3 + n
                    low = jnp.where(tile_id == t, window[at], low)
                    t += 1
        pos = key_table[n:n + 1, :]
        if n == 0:
            pos = pos + z * frames
        term = (pos >= low) & (pos < low + WIN)
        ok = term if ok is None else ok & term
    bias[:, :ext] = jnp.where(ok, F32(0), F32(-jnp.inf))
    place = lax.broadcasted_iota(jnp.int32, (rows, txt), 1)
    bias[:, ext:] = jnp.where(place < count[0], F32(0), F32(-jnp.inf))

    locals_[0].wait()
    locals_[6].wait()

    def term_of(xs):
        return contract(gfull[xs], w[row_block(xs, slot), :], ((1,), (0,)))

    total = term_of(x)
    for step in range(1, nx):
        xs = lax.rem(x + nx - step, nx)
        got(gfull.at[xs], og_s.at[step], og_r.at[step])
    per_slot = slot // chunk
    for j in range(2 * nz):
        stage[j] = gfull[j // per_slot, :, (j % per_slot) * chunk:(j % per_slot + 1) * chunk]
    for step in range(1, nz):
        for ct in range(2):
            zt = lax.rem(z + step, nz)
            send(None, lambda zt=zt, step=step, ct=ct: copy(
                stage.at[zt * 2 + ct], a_all.at[z, row_block(c, rows), :], a_s.at[step, ct], a_r.at[step, c],
                (y, zt, x, ct)))
    send(None, lambda: copy(stage.at[z * 2 + 1 - c], a_all.at[z, row_block(c, rows), :], a_s.at[0, 0], a_r.at[0, c],
                            partner))
    a_all[z, row_block(c, rows), :] = stage[z * 2 + c]

    for slab, there, cond in ((0, 0, has_down), (2, 1, has_up)):
        @pl.when(cond)
        def _():
            for n, dst in enumerate((k_ext, v_ext)):
                got(dst.at[key_rows(c, slab)], kv_s.at[there, n], kv_r.at[there, n])
        for n, dst in enumerate((k_ext, v_ext)):
            send(cond, lambda n=n, dst=dst, slab=slab: copy(
                dst.at[key_rows(c, slab)], dst.at[key_rows(c, slab)], kp_s.at[slab, n], kp_r.at[slab, n], partner))

    for step in range(1, nx):
        total = total + term_of(lax.rem(x + nx - step, nx))
    do[...] = total.astype(BF16)

    for n in range(1, 6):
        locals_[n].wait()
    for slab, cond in ((0, has_down), (1, None), (2, has_up)):
        def arrive(slab=slab):
            for n, dst in enumerate((k_ext, v_ext)):
                got(dst.at[key_rows(1 - c, slab)], kp_s.at[slab, n], kp_r.at[slab, n])
        if cond is None:
            arrive()
        else:
            pl.when(cond)(arrive)

    def reduce_group(g):
        lanes = pl.ds(g * gcols, gcols)
        for n, (part, have, mid, summed, ret) in enumerate((
                (dk_part, k_got, k_mid, k_sum, k_ret), (dv_part, v_got, v_mid, v_sum, v_ret))):
            got(have.at[:, lanes], pr_s.at[g, n], pr_r.at[g, n])
            for slab in range(3):
                value = (part[key_rows(c, slab), lanes].astype(F32)
                         + have[pl.ds(slab * rows, rows), lanes].astype(F32))
                if slab == 1:
                    mid[:, lanes] = value
                else:
                    summed[slab // 2, :, lanes] = value.astype(BF16)
            send(has_down, lambda n=n, summed=summed, ret=ret: copy(
                summed.at[0, :, lanes], ret.at[1, :, lanes], rz_s.at[0, g, n], rz_r.at[0, g, n], down))
            send(has_up, lambda n=n, summed=summed, ret=ret: copy(
                summed.at[1, :, lanes], ret.at[0, :, lanes], rz_s.at[1, g, n], rz_r.at[1, g, n], up))

    for g in range(groups):
        for h in range(g * per, (g + 1) * per):
            at = pl.ds(h * HDIM, HDIM)
            qh, doh, kh, vh, tkh, tvh = q[:, at], do[:, at], k_ext[:, at], v_ext[:, at], tk[:, at], tv[:, at]
            s_w = contract(qh, kh, ((1,), (1,))) * scale + bias[:, :ext]
            s_t = contract(qh, tkh, ((1,), (1,))) * scale + bias[:, ext:]
            top = jnp.maximum(jnp.max(s_w, axis=1, keepdims=True), jnp.max(s_t, axis=1, keepdims=True))
            e_w = jnp.exp(s_w - top)
            e_t = jnp.exp(s_t - top)
            inv = 1.0 / (jnp.sum(e_w, axis=1, keepdims=True) + jnp.sum(e_t, axis=1, keepdims=True))
            p_w = e_w * inv
            p_t = e_t * inv
            pb_w = p_w.astype(BF16)
            pb_t = p_t.astype(BF16)
            oh = (contract(pb_w, vh, ((1,), (0,))) + contract(pb_t, tvh, ((1,), (0,)))).astype(BF16)
            o_all[z, row_block(c, rows), at] = oh
            delta = jnp.sum(doh.astype(F32) * oh.astype(F32), axis=1, keepdims=True)
            ds_w = (p_w * (contract(doh, vh, ((1,), (1,))) - delta)).astype(BF16)
            ds_t = (p_t * (contract(doh, tvh, ((1,), (1,))) - delta)).astype(BF16)
            dq = contract(ds_w, kh, ((1,), (0,))) + contract(ds_t, tkh, ((1,), (0,)))
            dq_out[:, at] = (dq * scale).astype(BF16)
            dk_part[:, at] = (contract(ds_w, qh, ((0,), (0,))) * scale).astype(BF16)
            dv_part[:, at] = contract(pb_w, doh, ((0,), (0,))).astype(BF16)
            t_part[0, :, at] = (contract(ds_t, qh, ((0,), (0,))) * scale).astype(BF16)
            t_part[1, :, at] = contract(pb_t, doh, ((0,), (0,))).astype(BF16)
        lanes = pl.ds(g * gcols, gcols)
        for n, (part, have) in enumerate(((dk_part, k_got), (dv_part, v_got))):
            send(None, lambda n=n, part=part, have=have, g=g, lanes=lanes: copy(
                part.at[row_block(1 - c, 3 * rows), lanes], have.at[:, lanes], pr_s.at[g, n], pr_r.at[g, n], partner))
        for step in range(nz):
            zt, dev = seq_peer(step)
            mine = o_all.at[z, row_block(c, rows), lanes]
            if step:
                send(None, lambda mine=mine, g=g, step=step, dev=dev: copy(
                    mine, mine, o_s.at[g, step], o_r.at[g, step], dev))
            else:
                send(None, lambda mine=mine, g=g: copy(mine, mine, of_s.at[g, 0], of_r.at[g, 0], partner))
        if g:
            reduce_group(g - 1)

    send(None, lambda: copy(t_part.at[1 - c], t_got, tp_s, tp_r, partner))
    reduce_group(groups - 1)
    got(t_got, tp_s, tp_r)
    t_sum[...] = (t_part[c].astype(F32) + t_got[...].astype(F32)).astype(BF16)
    for step in range(1, nz):
        zt, dev = seq_peer(step)
        send(None, lambda step=step, zt=zt, dev=dev: copy(
            t_sum.at[row_block(zt, share)], t_red.at[row_block(z, share)], ts_s.at[step], ts_r.at[step], dev))

    for step in range(1, nz):
        zf = lax.rem(z + nz - step, nz)
        for g in range(groups):
            lanes = pl.ds(g * gcols, gcols)
            theirs = o_all.at[zf, row_block(c, rows), lanes]
            got(theirs, o_s.at[g, step], o_r.at[g, step])
            send(None, lambda theirs=theirs, g=g, step=step: copy(
                theirs, theirs, of_s.at[g, step], of_r.at[g, step], partner))

    value = t_sum[row_block(z, share), :].astype(F32)
    for step in range(1, nz):
        zf = lax.rem(z + nz - step, nz)
        got(t_red.at[row_block(zf, share)], ts_s.at[step], ts_r.at[step])
        value = value + t_red[row_block(zf, share), :].astype(F32)
    t_all[c, row_block(z, share), :] = value.astype(BF16)
    own_text = t_all.at[c, row_block(z, share)]
    for step in range(nz):
        zt, dev = seq_peer(step)
        if step:
            send(None, lambda step=step, dev=dev: copy(own_text, own_text, tg_s.at[step], tg_r.at[step], dev))
        else:
            send(None, lambda: copy(own_text, own_text, tf_s.at[0], tf_r.at[0], partner))

    for step in range(nz):
        zf = lax.rem(z + nz - step, nz)
        if step == 0:
            got(a_all.at[z, row_block(1 - c, rows), :], a_s.at[0, 0], a_r.at[0, 1 - c])
        else:
            for cf in range(2):
                got(a_all.at[zf, pl.ds(cf * rows, rows), :], a_s.at[step, cf], a_r.at[step, cf])
        for g in range(groups):
            got(o_all.at[zf, row_block(1 - c, rows), pl.ds(g * gcols, gcols)], of_s.at[g, step], of_r.at[g, step])
        part = contract(a_all[zf], o_all[zf], ((0,), (0,)))
        if step == 0:
            gw_out[...] = part
        else:
            gw_out[...] += part

    for slab, there, cond in ((0, 1, has_down), (1, 0, has_up)):
        @pl.when(cond)
        def _():
            for g in range(groups):
                for n, ret in enumerate((k_ret, v_ret)):
                    got(ret.at[slab, :, pl.ds(g * gcols, gcols)], rz_s.at[there, g, n], rz_r.at[there, g, n])
    for out, mid, ret in ((dk_out, k_mid, k_ret), (dv_out, v_mid, v_ret)):
        out[...] = (mid[...] + ret[0].astype(F32) + ret[1].astype(F32)).astype(BF16)

    for step in range(1, nz):
        zf = lax.rem(z + nz - step, nz)
        theirs = t_all.at[c, row_block(zf, share)]
        got(theirs, tg_s.at[step], tg_r.at[step])
        send(None, lambda theirs=theirs, step=step: copy(theirs, theirs, tf_s.at[step], tf_r.at[step], partner))
    for step in range(nz):
        zf = lax.rem(z + nz - step, nz)
        got(t_all.at[1 - c, row_block(zf, share)], tf_s.at[step], tf_r.at[step])
    dtk_out[...] = t_all[0].astype(F32)
    dtv_out[...] = t_all[1].astype(F32)

    for when, make in sent:
        if when is None:
            make().wait_send()
        else:
            pl.when(when)(lambda make=make: make().wait_send())


def per_device(
    mesh_shape, queries, key_rows, value_rows, out_grad, w_out, text_keys, text_values, text_count, window_start
):
    frames, height, width, cols = queries.shape
    rows = frames * height * width
    nz, nx = mesh_shape["seq"], mesh_shape["head"]
    txt = text_keys.shape[0]
    heads = cols // HDIM
    groups = min(4, heads)
    model = w_out.shape[0]
    chunk = model // (2 * nz)
    key = np.arange(6 * rows)
    block, inner = key // rows, key % rows
    half, slab = block // 3, block % 3
    table = np.zeros((8, 6 * rows), np.int32)
    table[0] = (slab - 1) * frames + inner // (height * width)
    table[1] = (half * height + inner // width % height) // TH
    table[2] = inner % width // TW
    own = np.arange(rows)
    tiles_w = width // TW
    tile = (own // (height * width) * (height // TH) + own // width % height // TH) * tiles_w + own % width // TW
    tile = tile.astype(np.int32)[:, None]
    dma = pltpu.SemaphoreType.DMA
    vmem = pltpu.VMEM
    anywhere = pl.BlockSpec(memory_space=pl.ANY)
    in_vmem = pl.BlockSpec(memory_space=pltpu.VMEM)
    in_smem = pl.BlockSpec(memory_space=pltpu.SMEM)
    flat = (rows, cols)
    cfg = (nz, nx, rows, cols, groups, frames, height, width)
    out = pl.pallas_call(
        functools.partial(body, cfg),
        in_specs=[in_smem, in_smem, in_vmem, in_vmem] + [anywhere] * 7,
        out_specs=[in_vmem] * 6,
        out_shape=[
            jax.ShapeDtypeStruct(flat, BF16), jax.ShapeDtypeStruct(flat, BF16), jax.ShapeDtypeStruct(flat, BF16),
            jax.ShapeDtypeStruct((chunk, cols), F32),
            jax.ShapeDtypeStruct((txt, cols), F32), jax.ShapeDtypeStruct((txt, cols), F32),
        ],
        scratch_shapes=[
            vmem(flat, BF16), vmem((txt, cols), BF16), vmem((txt, cols), BF16), vmem((model, cols), BF16),
            vmem(flat, BF16), vmem((rows, 6 * rows + txt), F32),
            vmem((nx, rows, model // nx), BF16), vmem((2 * nz, rows, chunk), BF16), vmem((nz, 2 * rows, chunk), BF16),
            vmem((6 * rows, cols), BF16), vmem((6 * rows, cols), BF16),
            vmem((6 * rows, cols), BF16), vmem((6 * rows, cols), BF16),
            vmem((3 * rows, cols), BF16), vmem((3 * rows, cols), BF16),
            vmem((2, rows, cols), BF16), vmem((2, rows, cols), BF16),
            vmem(flat, F32), vmem(flat, F32),
            vmem((2, rows, cols), BF16), vmem((2, rows, cols), BF16),
            vmem((nz, 2 * rows, cols), BF16),
            vmem((2, txt, cols), BF16), vmem((txt, cols), BF16), vmem((txt, cols), BF16), vmem((txt, cols), BF16),
            vmem((2, txt, cols), BF16),
            dma((7,)), dma((nx,)), dma((nx,)), dma((2, 2)), dma((2, 2)), dma((3, 2)), dma((3, 2)),
            dma((nz, 2)), dma((nz, 2)), dma((groups, 2)), dma((groups, 2)), dma((2, groups, 2)), dma((2, groups, 2)),
            dma((groups, nz)), dma((groups, nz)), dma((groups, nz)), dma((groups, nz)),
            dma, dma, dma((nz,)), dma((nz,)), dma((nz,)), dma((nz,)), dma((nz,)), dma((nz,)),
        ],
        compiler_params=pltpu.CompilerParams(
            collective_id=0, has_side_effects=True, vmem_limit_bytes=62 * 1024 * 1024),
        name="sta_backward",
    )(window_start.reshape(-1), text_count, jnp.asarray(table), jnp.asarray(tile),
      queries.reshape(flat), key_rows.reshape(flat), value_rows.reshape(flat), out_grad.reshape(rows, -1),
      w_out, text_keys, text_values)
    dq, dk, dv, gw, dtk, dtv = out
    return dq.reshape(queries.shape), dk.reshape(queries.shape), dv.reshape(queries.shape), gw, dtk, dtv


def solution(mesh):
    tok = P(("parts", "seq"), "hgt", None, "head")
    return jax.shard_map(
        functools.partial(per_device, dict(mesh.shape)),
        mesh=mesh,
        in_specs=(tok, tok, tok, tok, P(None, "head"), P("parts", "head"), P("parts", "head"),
                  P("parts"), P("parts", None, None, None)),
        out_specs=(tok, tok, tok, P(("parts", "seq", "hgt"), "head"), P("parts", "head"), P("parts", "head")),
        check_vma=False,
    )
```

time: 223 us -> 140 us (0.63)
  waiting for transfers between devices: 128 us -> 0 us
  Pallas kernels: 15.5 us -> 126 us
  starting transfers between devices: 29.7 us -> 0 us
  other arithmetic: 13.8 us -> 0 us
  between operations: 14.7 us -> 1.3 us
  matrix products: 8.71 us -> 0 us
    pallas_call x1, Pallas kernels: 15.5 us -> 126 us  [per_device(): pl.pallas_call(functools.partial(body, cfg), in_specs=[in_smem, in_smem,...]
    ppermute x10 -> x0, waiting for transfers between devices: 62.7 us -> none  [the longest x2 41.2 us: back(): low = lax.ppermute(mine[0].astype(BF16), 'seq', down)]
    psum x1 -> x0, waiting for transfers between devices: 54.3 us -> none  [per_device(): grad_text_key, grad_text_value = lax.psum((dtk, dtv), ('seq', 'hgt'))]
    ppermute x10 -> x0, starting transfers between devices: 24.7 us -> none  [the longest x2 10.6 us: back(): high = lax.ppermute(mine[2].astype(BF16), 'seq', up)]
    all_gather x4 -> x0, waiting for transfers between devices: 10.4 us -> none  [the longest x2 10.4 us: halo(): lax.all_gather(slabs, 'hgt', axis=1).reshape(3 * halves * rows, columns)]
    another operation x4 -> x0, other arithmetic: 8.78 us -> none
    dot_general x2 -> x0, matrix products: 8.71 us -> none  [the longest x1 4.63 us: per_device(): grad_o = jnp.dot(grad_full, w_out, preferred_element_type=F32).astype(BF16)]
    all_to_all x1 -> x0, starting transfers between devices: 4.86 us -> none  [per_device(): lax.all_to_all(grad_full, ('seq', 'hgt'), split_axis=1, concat_axis=0, ti...]
  transfers between devices with their start and end apart: 16 -> 0, of which waited for: 8 -> 0; matrix products, arithmetic and copies ran while one was open for 13% -> 0% of each run, Pallas kernels for 0% -> 0%
where the time goes in v2:
time: 140 us; the launch traced here: 138 us
  Pallas kernels  126 us (90%)
  local copies, waits for them, and re-layouts  11.4 us (8%)
    pallas_call x1, Pallas kernels, per_device(): pl.pallas_call(functools.partial(body, cfg), in_specs=[in_smem, in_smem,...  126 us
    unnamed x13, local copies, waits for them, and re-layouts  10.7 us

profile of v2, /device:TPU:0, one launch (start us, length us, event | category | flops | bytes accessed | tf_op | source)
XLA Modules:
  0.0 138.4 jit_solution(2719866062973004012)
XLA Ops:
  1.3 0.9 copy.17
  2.1 0.8 reshape.36.window
  2.9 125.7 %sta_backward.1 = (bf16[192,1024]{1,0:T(8,128)(2,1)}, bf16[192,1024]{1,0:T(8,128)(2,1)}, bf16[192,1024]{1,0:T(8,128)(2,1)}, f32[384,1024]{1,0:T(8,128)}, f32[256,1024]{1,0:T(8,128)}, /*index=5*/f32[256,1024]{1,0:T(8,128)}) custom-call(s32[288]{0:T(512)} %reshape.36.window, s32[1]{0:T(128)S(6)} %copy.24.count, s32[8,1152]{1,0:T(8,128)} %constant.4.clone.key_table, ...), custom_call_target="tpu_custom_call" | custom-call | tf_op jit(solution)/shard_map/sta_backward/pallas_call | solution.py:353
  128.6 0.0 copy-start
  128.7 1.9 %copy.25 = bf16[2,4,24,1024]{3,2,1,0:T(8,128)(2,1)} copy(bf16[2,4,24,1024]{3,2,1,0:T(8,128)(2,1)} %bitcast.13) | data formatting | bytes 786432
  130.5 1.8 %copy.26 = bf16[2,4,24,1024]{3,2,1,0:T(8,128)(2,1)} copy(bf16[2,4,24,1024]{3,2,1,0:T(8,128)(2,1)} %bitcast.12) | data formatting | bytes 786432
  132.3 1.8 %copy.27 = bf16[2,4,24,1024]{3,2,1,0:T(8,128)(2,1)} copy(bf16[2,4,24,1024]{3,2,1,0:T(8,128)(2,1)} %bitcast.11) | data formatting | bytes 786432
  134.1 0.0 copy-done
  134.1 0.0 copy-start.2
  134.1 1.1 copy.28
  135.2 0.6 copy-done.2
  135.9 0.0 copy-start.1
  135.9 1.0 copy.29
  136.8 0.6 copy-done.1
  137.5 1.0 copy.30
Async XLA Ops:
  128.6 5.4 %copy-start = (f32[384,1024]{1,0:T(8,128)S(1)}, f32[384,1024]{1,0:T(8,128)}, u32[]{:S(2)}) copy-start(f32[384,1024]{1,0:T(8,128)} %get-tuple-element.27) | copy-start | bytes 4718596
  134.1 1.8 %copy-start.2 = (f32[256,1024]{1,0:T(8,128)S(1)}, f32[256,1024]{1,0:T(8,128)}, u32[]{:S(2)}) copy-start(f32[256,1024]{1,0:T(8,128)} %get-tuple-element.28) | copy-start | bytes 3145732
  135.9 1.6 %copy-start.1 = (f32[256,1024]{1,0:T(8,128)S(1)}, f32[256,1024]{1,0:T(8,128)}, u32[]{:S(2)}) copy-start(f32[256,1024]{1,0:T(8,128)} %get-tuple-element.29) | copy-start | bytes 3145732

commit v3 on v2

--- a/solution.py
+++ b/solution.py
@@ -26,7 +26,7 @@
          dq_out, dk_out, dv_out, gw_out, dtk_out, dtv_out,
          q, tk, tv, w, do, bias, gfull, stage, a_all, k_ext, v_ext, dk_part, dv_part, k_got, v_got,
          k_sum, v_sum, k_mid, v_mid, k_ret, v_ret, o_all, t_part, t_got, t_sum, t_red, t_all,
-         loc, og_s, og_r, kv_s, kv_r, kp_s, kp_r, a_s, a_r, pr_s, pr_r, rz_s, rz_r,
+         loc, og_s, og_r, kv_s, kv_r, kp_s, kp_r, a_s, a_r, ax_s, ax_r, pr_s, pr_r, rz_s, rz_r,
          o_s, o_r, of_s, of_r, tp_s, tp_r, ts_s, ts_r, tg_s, tg_r, tf_s, tf_r):
     nz, nx, rows, cols, groups, frames, height, width = cfg
     txt = tk_in.shape[0]
@@ -42,6 +42,10 @@
     partner = (y, z, x, 1 - c)
     up = (y, lax.rem(z + 1, nz), x, c)
     down = (y, lax.rem(z + nz - 1, nz), x, c)
+    split = 2 if nx % 2 == 0 else 1
+    piece = rows // split
+    x_half = lax.rem(x, split)
+    x_partner = (y, z, x + 1 - 2 * x_half, c)
     has_up = z < nz - 1
     has_down = z > 0
 
@@ -61,6 +65,9 @@
 
     def key_rows(half, slab):
         return row_block(half * 3 + slab, rows)
+
+    def a_piece(zf, cf, n):
+        return a_all.at[zf, pl.ds(pl.multiple_of(cf * rows + n * piece, 16), piece), :]
 
     sent = []
 
@@ -160,8 +167,8 @@
         for ct in range(2):
             zt = lax.rem(z + step, nz)
             send(None, lambda zt=zt, step=step, ct=ct: copy(
-                stage.at[zt * 2 + ct], a_all.at[z, row_block(c, rows), :], a_s.at[step, ct], a_r.at[step, c],
-                (y, zt, x, ct)))
+                stage.at[zt * 2 + ct, row_block(x_half, piece), :], a_piece(z, c, x_half), a_s.at[step, ct],
+                a_r.at[step, c], (y, zt, x, ct)))
     send(None, lambda: copy(stage.at[z * 2 + 1 - c], a_all.at[z, row_block(c, rows), :], a_s.at[0, 0], a_r.at[0, c],
                             partner))
     a_all[z, row_block(c, rows), :] = stage[z * 2 + c]
@@ -206,6 +213,15 @@
                 summed.at[0, :, lanes], ret.at[1, :, lanes], rz_s.at[0, g, n], rz_r.at[0, g, n], down))
             send(has_up, lambda n=n, summed=summed, ret=ret: copy(
                 summed.at[1, :, lanes], ret.at[0, :, lanes], rz_s.at[1, g, n], rz_r.at[1, g, n], up))
+
+    def share_pieces(step):
+        zf = lax.rem(z + nz - step, nz)
+        for cf in range(2):
+            theirs = a_piece(zf, cf, x_half)
+            got(theirs, a_s.at[step, cf], a_r.at[step, cf])
+            if split > 1:
+                send(None, lambda theirs=theirs, cf=cf: copy(
+                    theirs, theirs, ax_s.at[step, cf], ax_r.at[step, cf], x_partner))
 
     for g in range(groups):
         for h in range(g * per, (g + 1) * per):
@@ -246,6 +262,9 @@
                 send(None, lambda mine=mine, g=g: copy(mine, mine, of_s.at[g, 0], of_r.at[g, 0], partner))
         if g:
             reduce_group(g - 1)
+        for step in range(1, nz):
+            if g == min(step, groups - 1):
+                share_pieces(step)
 
     send(None, lambda: copy(t_part.at[1 - c], t_got, tp_s, tp_r, partner))
     reduce_group(groups - 1)
@@ -256,14 +275,30 @@
         send(None, lambda step=step, zt=zt, dev=dev: copy(
             t_sum.at[row_block(zt, share)], t_red.at[row_block(z, share)], ts_s.at[step], ts_r.at[step], dev))
 
-    for step in range(1, nz):
-        zf = lax.rem(z + nz - step, nz)
+    def share_o(g, step):
+        zf = lax.rem(z + nz - step, nz)
+        theirs = o_all.at[zf, row_block(c, rows), pl.ds(g * gcols, gcols)]
+        got(theirs, o_s.at[g, step], o_r.at[g, step])
+        send(None, lambda: copy(theirs, theirs, of_s.at[g, step], of_r.at[g, step], partner))
+
+    def project(step):
+        zf = lax.rem(z + nz - step, nz)
+        if step == 0:
+            got(a_all.at[z, row_block(1 - c, rows), :], a_s.at[0, 0], a_r.at[0, 1 - c])
+        elif split > 1:
+            for cf in range(2):
+                got(a_piece(zf, cf, 1 - x_half), ax_s.at[step, cf], ax_r.at[step, cf])
         for g in range(groups):
-            lanes = pl.ds(g * gcols, gcols)
-            theirs = o_all.at[zf, row_block(c, rows), lanes]
-            got(theirs, o_s.at[g, step], o_r.at[g, step])
-            send(None, lambda theirs=theirs, g=g, step=step: copy(
-                theirs, theirs, of_s.at[g, step], of_r.at[g, step], partner))
+            got(o_all.at[zf, row_block(1 - c, rows), pl.ds(g * gcols, gcols)], of_s.at[g, step], of_r.at[g, step])
+        part = contract(a_all[zf], o_all[zf], ((0,), (0,)))
+        if step == 0:
+            gw_out[...] = part
+        else:
+            gw_out[...] += part
+
+    for g in range(groups - 1):
+        for step in range(1, nz):
+            share_o(g, step)
 
     value = t_sum[row_block(z, share), :].astype(F32)
     for step in range(1, nz):
@@ -279,20 +314,11 @@
         else:
             send(None, lambda: copy(own_text, own_text, tf_s.at[0], tf_r.at[0], partner))
 
-    for step in range(nz):
-        zf = lax.rem(z + nz - step, nz)
-        if step == 0:
-            got(a_all.at[z, row_block(1 - c, rows), :], a_s.at[0, 0], a_r.at[0, 1 - c])
-        else:
-            for cf in range(2):
-                got(a_all.at[zf, pl.ds(cf * rows, rows), :], a_s.at[step, cf], a_r.at[step, cf])
-        for g in range(groups):
-            got(o_all.at[zf, row_block(1 - c, rows), pl.ds(g * gcols, gcols)], of_s.at[g, step], of_r.at[g, step])
-        part = contract(a_all[zf], o_all[zf], ((0,), (0,)))
-        if step == 0:
-            gw_out[...] = part
-        else:
-            gw_out[...] += part
+    project(0)
+    for step in range(1, nz):
+        share_o(groups - 1, step)
+    for step in range(1, nz):
+        project(step)
 
     for slab, there, cond in ((0, 1, has_down), (1, 0, has_up)):
         @pl.when(cond)
@@ -319,6 +345,28 @@
             make().wait_send()
         else:
             pl.when(when)(lambda make=make: make().wait_send())
+
+
+def deliver_body(*refs):
+    sems = refs[-1]
+    count = (len(refs) - 1) // 2
+    copies = [pltpu.make_async_copy(refs[n], refs[count + n], sems.at[n]) for n in range(count)]
+    for one in copies:
+        one.start()
+    for one in copies:
+        one.wait()
+
+
+def deliver(arrays):
+    anywhere = pl.BlockSpec(memory_space=pl.ANY)
+    return pl.pallas_call(
+        deliver_body,
+        in_specs=[anywhere] * len(arrays),
+        out_specs=[anywhere] * len(arrays),
+        out_shape=[jax.ShapeDtypeStruct(a.shape, a.dtype) for a in arrays],
+        scratch_shapes=[pltpu.SemaphoreType.DMA((len(arrays),))],
+        name="deliver",
+    )(*arrays)
 
 
 def per_device(
@@ -373,7 +421,7 @@
             vmem((2, txt, cols), BF16), vmem((txt, cols), BF16), vmem((txt, cols), BF16), vmem((txt, cols), BF16),
             vmem((2, txt, cols), BF16),
             dma((7,)), dma((nx,)), dma((nx,)), dma((2, 2)), dma((2, 2)), dma((3, 2)), dma((3, 2)),
-            dma((nz, 2)), dma((nz, 2)), dma((groups, 2)), dma((groups, 2)), dma((2, groups, 2)), dma((2, groups, 2)),
+            dma((nz, 2)), dma((nz, 2)), dma((nz, 2)), dma((nz, 2)), dma((groups, 2)), dma((groups, 2)), dma((2, groups, 2)), dma((2, groups, 2)),
             dma((groups, nz)), dma((groups, nz)), dma((groups, nz)), dma((groups, nz)),
             dma, dma, dma((nz,)), dma((nz,)), dma((nz,)), dma((nz,)), dma((nz,)), dma((nz,)),
         ],
@@ -383,7 +431,7 @@
     )(window_start.reshape(-1), text_count, jnp.asarray(table), jnp.asarray(tile),
       queries.reshape(flat), key_rows.reshape(flat), value_rows.reshape(flat), out_grad.reshape(rows, -1),
       w_out, text_keys, text_values)
-    dq, dk, dv, gw, dtk, dtv = out
+    dq, dk, dv, gw, dtk, dtv = deliver(out)
     return dq.reshape(queries.shape), dk.reshape(queries.shape), dv.reshape(queries.shape), gw, dtk, dtv
 
 

time: 140 us -> 266 us (1.90)
  Pallas kernels: 126 us -> 261 us
  local copies, waits for them, and re-layouts: 11.4 us -> 1.63 us
    pallas_call x0 -> x1, Pallas kernels: none -> 148 us  [deliver(): pl.pallas_call(deliver_body, in_specs=[anywhere] * len(arrays), out_specs...]
    pallas_call x1, Pallas kernels: 126 us -> 113 us  [per_device(): pl.pallas_call(functools.partial(body, cfg), in_specs=[in_smem, in_smem,...]
    unnamed x13 -> x1, local copies, waits for them, and re-layouts: 10.7 us -> 0.87 us
where the time goes in v3:
time: 266 us; the launch traced here: 264 us
  Pallas kernels  261 us (98%)
    pallas_call x1, Pallas kernels, deliver(): pl.pallas_call(deliver_body, in_specs=[anywhere] * len(arrays), out_specs...  148 us
    pallas_call x1, Pallas kernels, per_device(): pl.pallas_call(functools.partial(body, cfg), in_specs=[in_smem, in_smem,...  113 us

profile of v3, /device:TPU:0, one launch (start us, length us, event | category | flops | bytes accessed | tf_op | source)
XLA Modules:
  0.0 263.8 jit_solution(17248793528050886504)
XLA Ops:
  1.3 0.9 copy.17
  2.1 0.8 reshape.36.window
  2.9 112.7 %sta_backward.1 = (bf16[192,1024]{1,0:T(8,128)(2,1)}, bf16[192,1024]{1,0:T(8,128)(2,1)}, bf16[192,1024]{1,0:T(8,128)(2,1)}, f32[384,1024]{1,0:T(8,128)}, f32[256,1024]{1,0:T(8,128)}, /*index=5*/f32[256,1024]{1,0:T(8,128)}) custom-call(s32[288]{0:T(512)} %reshape.36.window, s32[1]{0:T(128)S(6)} %copy.18.count, s32[8,1152]{1,0:T(8,128)} %constant.4.clone.key_table, ...), custom_call_target="tpu_custom_call" | custom-call | tf_op jit(solution)/shard_map/sta_backward/pallas_call | solution.py:401
  115.6 148.1 %deliver.1 = (bf16[192,1024]{1,0:T(8,128)(2,1)}, bf16[192,1024]{1,0:T(8,128)(2,1)}, bf16[192,1024]{1,0:T(8,128)(2,1)}, f32[384,1024]{1,0:T(8,128)}, f32[256,1024]{1,0:T(8,128)}, /*index=5*/f32[256,1024]{1,0:T(8,128)}) custom-call(bf16[192,1024]{1,0:T(8,128)(2,1)} %get-tuple-element.18.refs_0_, bf16[192,1024]{1,0:T(8,128)(2,1)} %get-tuple-element.19.refs_1_, ...), custom_call_target="tpu_custom_call" | custom-call | tf_op jit(solution)/shard_map/deliver/pallas_call | solution.py:362

commit v4 on v3

--- a/solution.py
+++ b/solution.py
@@ -348,23 +348,30 @@
 
 
 def deliver_body(*refs):
-    sems = refs[-1]
-    count = (len(refs) - 1) // 2
-    copies = [pltpu.make_async_copy(refs[n], refs[count + n], sems.at[n]) for n in range(count)]
-    for one in copies:
+    count = (len(refs) - 2) // 3
+    source, target, held = refs[:count], refs[count:2 * count], refs[2 * count:3 * count]
+    in_sem, out_sem = refs[-2:]
+    come = [pltpu.make_async_copy(source[n], held[n], in_sem.at[n]) for n in range(count)]
+    go = [pltpu.make_async_copy(held[n], target[n], out_sem.at[n]) for n in range(count)]
+    for one in come:
         one.start()
-    for one in copies:
+    for n in range(count):
+        come[n].wait()
+        go[n].start()
+    for one in go:
         one.wait()
 
 
 def deliver(arrays):
     anywhere = pl.BlockSpec(memory_space=pl.ANY)
+    sems = pltpu.SemaphoreType.DMA((len(arrays),))
     return pl.pallas_call(
         deliver_body,
         in_specs=[anywhere] * len(arrays),
         out_specs=[anywhere] * len(arrays),
         out_shape=[jax.ShapeDtypeStruct(a.shape, a.dtype) for a in arrays],
-        scratch_shapes=[pltpu.SemaphoreType.DMA((len(arrays),))],
+        scratch_shapes=[pltpu.VMEM(a.shape, a.dtype) for a in arrays] + [sems, sems],
+        compiler_params=pltpu.CompilerParams(vmem_limit_bytes=62 * 1024 * 1024),
         name="deliver",
     )(*arrays)
 

time: 266 us -> 122 us (0.46)
  Pallas kernels: 261 us -> 117 us
    pallas_call x1, Pallas kernels: 148 us -> 4.09 us  [deliver(): pl.pallas_call(deliver_body, in_specs=[anywhere] * len(arrays), out_specs...]
where the time goes in v4:
time: 122 us; the launch traced here: 120 us
  Pallas kernels  117 us (96%)
  local copies, waits for them, and re-layouts  1.63 us (1%)
  between operations  1.45 us (1%)
    pallas_call x1, Pallas kernels, per_device(): pl.pallas_call(functools.partial(body, cfg), in_specs=[in_smem, in_smem,...  113 us
    pallas_call x1, Pallas kernels, deliver(): pl.pallas_call(deliver_body, in_specs=[anywhere] * len(arrays), out_specs...  4.09 us

profile of v4, /device:TPU:0, one launch (start us, length us, event | category | flops | bytes accessed | tf_op | source)
XLA Modules:
  0.0 119.8 jit_solution(9162047980044526244)
XLA Ops:
  1.3 0.9 copy.17
  2.1 0.8 reshape.36.window
  2.9 112.7 %sta_backward.1 = (bf16[192,1024]{1,0:T(8,128)(2,1)}, bf16[192,1024]{1,0:T(8,128)(2,1)}, bf16[192,1024]{1,0:T(8,128)(2,1)}, f32[384,1024]{1,0:T(8,128)}, f32[256,1024]{1,0:T(8,128)}, /*index=5*/f32[256,1024]{1,0:T(8,128)}) custom-call(s32[288]{0:T(512)} %reshape.36.window, s32[1]{0:T(128)S(6)} %copy.18.count, s32[8,1152]{1,0:T(8,128)} %constant.4.clone.key_table, ...), custom_call_target="tpu_custom_call" | custom-call | tf_op jit(solution)/shard_map/sta_backward/pallas_call | solution.py:408
  115.6 4.1 %deliver.1 = (bf16[192,1024]{1,0:T(8,128)(2,1)}, bf16[192,1024]{1,0:T(8,128)(2,1)}, bf16[192,1024]{1,0:T(8,128)(2,1)}, f32[384,1024]{1,0:T(8,128)}, f32[256,1024]{1,0:T(8,128)}, /*index=5*/f32[256,1024]{1,0:T(8,128)}) custom-call(bf16[192,1024]{1,0:T(8,128)(2,1)} %get-tuple-element.18.refs_0_, bf16[192,1024]{1,0:T(8,128)(2,1)} %get-tuple-element.19.refs_1_, ...), custom_call_target="tpu_custom_call" | custom-call | tf_op jit(solution)/shard_map/deliver/pallas_call | solution.py:368

commit v5 on v4

--- a/solution.py
+++ b/solution.py
@@ -25,7 +25,7 @@
 def body(cfg, window, count, key_table, tile_table, q_in, k_in, v_in, og_in, w_in, tk_in, tv_in,
          dq_out, dk_out, dv_out, gw_out, dtk_out, dtv_out,
          q, tk, tv, w, do, bias, gfull, stage, a_all, k_ext, v_ext, dk_part, dv_part, k_got, v_got,
-         k_sum, v_sum, k_mid, v_mid, k_ret, v_ret, o_all, t_part, t_got, t_sum, t_red, t_all,
+         k_sum, v_sum, k_mid, v_mid, k_ret, v_ret, o_all, t_part, t_got, t_sum, t_red, t_run, t_all,
          loc, og_s, og_r, kv_s, kv_r, kp_s, kp_r, a_s, a_r, ax_s, ax_r, pr_s, pr_r, rz_s, rz_r,
          o_s, o_r, of_s, of_r, tp_s, tp_r, ts_s, ts_r, tg_s, tg_r, tf_s, tf_r):
     nz, nx, rows, cols, groups, frames, height, width = cfg
@@ -270,10 +270,21 @@
     reduce_group(groups - 1)
     got(t_got, tp_s, tp_r)
     t_sum[...] = (t_part[c].astype(F32) + t_got[...].astype(F32)).astype(BF16)
-    for step in range(1, nz):
-        zt, dev = seq_peer(step)
-        send(None, lambda step=step, zt=zt, dev=dev: copy(
-            t_sum.at[row_block(zt, share)], t_red.at[row_block(z, share)], ts_s.at[step], ts_r.at[step], dev))
+    for way, first, beyond, dev in ((0, has_down, lambda j: z < j, up), (1, has_up, lambda j: z > j, down)):
+        for j in (range(nz - 1, 0, -1) if way == 0 else range(nz - 1)):
+            at = pl.ds(j * share, share)
+
+            @pl.when(beyond(j) & first)
+            def _():
+                got(t_red.at[way, at], ts_s.at[way, j], ts_r.at[way, j])
+                t_run[way, at, :] = (t_sum[at, :].astype(F32) + t_red[way, at, :].astype(F32)).astype(BF16)
+
+            @pl.when(beyond(j) & jnp.logical_not(first))
+            def _():
+                t_run[way, at, :] = t_sum[at, :]
+
+            send(beyond(j), lambda way=way, j=j, at=at, dev=dev: copy(
+                t_run.at[way, at], t_red.at[way, at], ts_s.at[way, j], ts_r.at[way, j], dev))
 
     def share_o(g, step):
         zf = lax.rem(z + nz - step, nz)
@@ -301,11 +312,18 @@
             share_o(g, step)
 
     value = t_sum[row_block(z, share), :].astype(F32)
-    for step in range(1, nz):
-        zf = lax.rem(z + nz - step, nz)
-        got(t_red.at[row_block(zf, share)], ts_s.at[step], ts_r.at[step])
-        value = value + t_red[row_block(zf, share), :].astype(F32)
-    t_all[c, row_block(z, share), :] = value.astype(BF16)
+    mine = row_block(z, share)
+    for way, cond in ((0, has_down), (1, has_up)):
+        @pl.when(cond)
+        def _():
+            got(t_red.at[way, mine], ts_s.at[way, z], ts_r.at[way, z])
+
+        @pl.when(jnp.logical_not(cond))
+        def _():
+            t_red[way, mine, :] = jnp.zeros((share, cols), BF16)
+
+        value = value + t_red[way, mine, :].astype(F32)
+    t_all[c, mine, :] = value.astype(BF16)
     own_text = t_all.at[c, row_block(z, share)]
     for step in range(nz):
         zt, dev = seq_peer(step)
@@ -425,12 +443,13 @@
             vmem(flat, F32), vmem(flat, F32),
             vmem((2, rows, cols), BF16), vmem((2, rows, cols), BF16),
             vmem((nz, 2 * rows, cols), BF16),
-            vmem((2, txt, cols), BF16), vmem((txt, cols), BF16), vmem((txt, cols), BF16), vmem((txt, cols), BF16),
+            vmem((2, txt, cols), BF16), vmem((txt, cols), BF16), vmem((txt, cols), BF16), vmem((2, txt, cols), BF16),
+            vmem((2, txt, cols), BF16),
             vmem((2, txt, cols), BF16),
             dma((7,)), dma((nx,)), dma((nx,)), dma((2, 2)), dma((2, 2)), dma((3, 2)), dma((3, 2)),
             dma((nz, 2)), dma((nz, 2)), dma((nz, 2)), dma((nz, 2)), dma((groups, 2)), dma((groups, 2)), dma((2, groups, 2)), dma((2, groups, 2)),
             dma((groups, nz)), dma((groups, nz)), dma((groups, nz)), dma((groups, nz)),
-            dma, dma, dma((nz,)), dma((nz,)), dma((nz,)), dma((nz,)), dma((nz,)), dma((nz,)),
+            dma, dma, dma((2, nz)), dma((2, nz)), dma((nz,)), dma((nz,)), dma((nz,)), dma((nz,)),
         ],
         compiler_params=pltpu.CompilerParams(
             collective_id=0, has_side_effects=True, vmem_limit_bytes=62 * 1024 * 1024),

time: 122 us -> 128 us (1.049)
  the two profiles are of different devices: /device:TPU:0 before, /device:TPU:31 now
where the time goes in v5:
time: 128 us
  Pallas kernels  125 us (98%)
  local copies, waits for them, and re-layouts  1.63 us (1%)
  between operations  1.45 us (1%)
    pallas_call x1, Pallas kernels, per_device(): pl.pallas_call(functools.partial(body, cfg), in_specs=[in_smem, in_smem,...  121 us
    pallas_call x1, Pallas kernels, deliver(): pl.pallas_call(deliver_body, in_specs=[anywhere] * len(arrays), out_specs...  4.09 us

profile of v5, /device:TPU:31, one launch (start us, length us, event | category | flops | bytes accessed | tf_op | source)
XLA Modules:
  0.0 127.9 jit_solution(6011145271800268290)
XLA Ops:
  1.3 0.9 copy.17
  2.1 0.8 reshape.36.window
  2.9 120.7 %sta_backward.1 = (bf16[192,1024]{1,0:T(8,128)(2,1)}, bf16[192,1024]{1,0:T(8,128)(2,1)}, bf16[192,1024]{1,0:T(8,128)(2,1)}, f32[384,1024]{1,0:T(8,128)}, f32[256,1024]{1,0:T(8,128)}, /*index=5*/f32[256,1024]{1,0:T(8,128)}) custom-call(s32[288]{0:T(512)} %reshape.36.window, s32[1]{0:T(128)S(6)} %copy.18.count, s32[8,1152]{1,0:T(8,128)} %constant.4.clone.key_table, ...), custom_call_target="tpu_custom_call" | custom-call | tf_op jit(solution)/shard_map/sta_backward/pallas_call | solution.py:426
  123.6 4.1 %deliver.1 = (bf16[192,1024]{1,0:T(8,128)(2,1)}, bf16[192,1024]{1,0:T(8,128)(2,1)}, bf16[192,1024]{1,0:T(8,128)(2,1)}, f32[384,1024]{1,0:T(8,128)}, f32[256,1024]{1,0:T(8,128)}, /*index=5*/f32[256,1024]{1,0:T(8,128)}) custom-call(bf16[192,1024]{1,0:T(8,128)(2,1)} %get-tuple-element.18.refs_0_, bf16[192,1024]{1,0:T(8,128)(2,1)} %get-tuple-element.19.refs_1_, ...), custom_call_target="tpu_custom_call" | custom-call | tf_op jit(solution)/shard_map/deliver/pallas_call | solution.py:386
